TPU v7x, 256 devices: a whole 4x4x8 slice. The times are simulated.
256 devices in a mesh: aux: 2 (over y_hi), blk: 128 (over z, y_lo, x, core).
Axes of the slice: x: 4, y: 4 (y_hi: 2, y_lo: 2; y = y_hi * 2 + y_lo), z: 8, core: 2. Of those that a mesh axis runs over, the one named last changes fastest.
Arguments:
- integrals: bfloat16 [8, 10240, 10240], P('aux', 'blk'), may hold values from -6 to 6
- coefficients: bfloat16 [10240, 256], P('blk'), may hold values from -0.0012207031 to 0.0012207031
Outputs:
- exchange_matrix: float32 [10240, 10240], P('blk', 'aux')
All inputs are finite; a program needn't handle non-finite values.
Results may differ from a plain program's by a relative error of at most 0.0037.
Values may be sent and summed in bfloat16 or wider, within the bound.
No kernel may reach another device: no remote copies, remote signals or barrier semaphores. Data moves between devices by JAX's collectives and lax.ppermute only.
A program may use at most 128 MiB of HBM per device.

v0:
```python
import jax
import jax.numpy as jnp
from jax import lax
from jax.sharding import PartitionSpec as P


def passed_along(array, axis, by):
    count = lax.axis_size(axis)
    return lax.ppermute(array, axis, [(i, (i + by) % count) for i in range(count)])


def put_tile(row_tiles, product, slot):
    return lax.dynamic_update_slice_in_dim(row_tiles, product[:, None, :], slot, 1)


def per_device(integrals, coefficients):
    aux_local = integrals.shape[0]
    row_count = integrals.shape[1]
    basis_size = integrals.shape[2]
    occ_count = coefficients.shape[1]
    flat_integrals = integrals.reshape(aux_local * row_count, basis_size)
    partial_value = jnp.dot(
        flat_integrals,
        lax.all_gather(coefficients, "blk", axis=0, tiled=True),
        preferred_element_type=jnp.float32,
    )
    halfway = partial_value.astype(jnp.bfloat16).reshape(aux_local, row_count, occ_count)
    local_rows = lax.all_to_all(halfway, "aux", split_axis=2, concat_axis=0, tiled=True)

    def tile_product(other):
        return jnp.einsum("pri,psi->rs", local_rows, other, preferred_element_type=jnp.float32)

    cycle_size = lax.axis_size("blk")
    own_index = lax.axis_index("blk")
    row_tiles = jnp.zeros((row_count, cycle_size, row_count), jnp.float32)
    row_tiles = put_tile(row_tiles, tile_product(local_rows), own_index)

    def full_step(offset, carry):
        travel, tiles_now = carry
        travel = passed_along(travel, "blk", 1)
        slot = (own_index - offset) % cycle_size
        return (travel, put_tile(tiles_now, tile_product(travel), slot))

    carried, row_tiles = lax.fori_loop(1, cycle_size, full_step, (local_rows, row_tiles))
    exchange_rows = row_tiles.reshape(row_count, cycle_size * row_count)
    return lax.psum_scatter(exchange_rows, "aux", scatter_dimension=1, tiled=True)


def solution(mesh):
    in_specs = (P("aux", "blk", None), P("blk", None))
    out_specs = P("blk", "aux")
    return jax.shard_map(
        per_device, mesh=mesh, in_specs=in_specs, out_specs=out_specs, check_vma=False
    )
```

profile of v0, /device:TPU:1, one launch (start us, length us, event | category | flops | bytes accessed | tf_op | source)
XLA Modules:
  0.0 1561.9 jit_solution(7908276973861039096)
XLA Ops:
  7.3 223.2 %all-gather.2.cloned.1.call-done = bf16[10240,256]{1,0:T(8,128)(2,1)} async-done(((bf16[80,256]{1,0:T(8,128)(2,1)}), bf16[10240,256]{1,0:T(8,128)(2,1)}) %all-gather.2.cloned.1.call-update) | async-done | bytes 5242896 | tf_op jit(solution)/shard_map/all_gather | solution.py:24
  250.1 1237.7 %while.17 = (s32[]{:T(128)}, bf16[8,80,128]{2,1,0:T(8,128)(2,1)S(1)}, f32[80,128,80]{2,0,1:T(8,128)}, bf16[8,80,128]{2,1,0:T(8,128)(2,1)S(1)}, s32[]{:T(128)}, /*index=5*/s32[]{:T(128)}, s32[]{:T(128)}, s32[]{:T(128)}, s32[]{:T(128)}) while((s32[]{:T(128)}, bf16[8,80,128]{2,1,0:T(8,128)(2,1)S(1)}, f32[80,128,80]{2,0,1:T(8,128)}, ...), condition=%wide.region_1.2_spmd, body=%wide.region_0.1_spmd.sunk | while | flops 13107217 | bytes 1351972 | solution.py:44
  322.9 9.0 collective-permute-done
  381.6 9.0 collective-permute-done
  420.8 9.0 collective-permute-done
  450.2 9.0 collective-permute-done
  479.5 9.0 collective-permute-done
  528.5 9.0 collective-permute-done
  557.8 9.0 collective-permute-done
  597.0 9.0 collective-permute-done
  645.9 9.0 collective-permute-done
  694.9 9.0 collective-permute-done
  704.7 9.0 collective-permute-done
  763.4 9.0 collective-permute-done
  773.2 9.0 collective-permute-done
  949.4 9.0 collective-permute-done
  969.0 9.0 collective-permute-done
  988.6 9.0 collective-permute-done
  1106.0 9.0 collective-permute-done
  1155.0 9.0 collective-permute-done
  1174.5 9.0 collective-permute-done
  1203.9 9.0 collective-permute-done
  1233.2 9.0 collective-permute-done
  1272.4 9.0 collective-permute-done
  1292.0 9.0 collective-permute-done
  1311.6 9.0 collective-permute-done
  1370.3 9.0 collective-permute-done
  1389.9 9.0 collective-permute-done
  1399.7 9.0 collective-permute-done
  1429.0 9.0 collective-permute-done
  1458.4 9.0 collective-permute-done
  1500.7 54.4 %reduce-scatter.2.cloned.1.call-done = f32[80,5120]{1,0:T(8,128)} async-done(((f32[80,10240]{1,0:T(8,128)}), f32[80,5120]{1,0:T(8,128)}) %reduce-scatter.2.cloned.1.call-update) | async-done | bytes 1638416 | tf_op jit(solution)/shard_map/reduce_scatter | solution.py:46
  (495 shorter events, 1010.1 us)
Async XLA Ops:
  6.5 223.9 %all-gather.2.cloned.1.call-start = ((), (), s32[]{:S(2)}) async-start(), calls=%async_computation.2 | async-start | bytes 5283840 | tf_op jit(solution)/shard_map/all_gather | solution.py:24
  237.6 9.5 all-to-all-start
  241.6 1313.5 %reduce-scatter.2.cloned.1.call-start = ((), (), s32[]{:S(2)}) async-start(), calls=%async_computation.3 | async-start | bytes 4915200 | tf_op jit(solution)/shard_map/reduce_scatter | solution.py:46
  322.9 9.0 collective-permute-start
  381.6 9.0 collective-permute-start
  420.8 9.0 collective-permute-start
  450.2 9.0 collective-permute-start
  479.5 9.0 collective-permute-start
  528.4 9.0 collective-permute-start
  557.8 9.0 collective-permute-start
  597.0 9.0 collective-permute-start
  645.9 9.0 collective-permute-start
  694.9 9.0 collective-permute-start
  704.7 9.0 collective-permute-start
  763.4 9.0 collective-permute-start
  773.2 9.0 collective-permute-start
  949.4 9.0 collective-permute-start
  969.0 9.0 collective-permute-start
  988.5 9.0 collective-permute-start
  1106.0 9.0 collective-permute-start
  1155.0 9.0 collective-permute-start
  1174.5 9.0 collective-permute-start
  1203.9 9.0 collective-permute-start
  1233.2 9.0 collective-permute-start
  1272.4 9.0 collective-permute-start
  1292.0 9.0 collective-permute-start
  1311.6 9.0 collective-permute-start
  1370.3 9.0 collective-permute-start
  1389.9 9.0 collective-permute-start
  1399.7 9.0 collective-permute-start
  1429.0 9.0 collective-permute-start
  1458.4 9.0 collective-permute-start
  (99 other events, 874.9 us)
Sparse Core Ops, SparseCore 0:
  9.2 221.2 all-gather.1
  1500.8 54.2 reduce-scatter.1
where the time goes:
time: 1560 us
  waiting for transfers between devices  1410 us (90%)
  matrix products  109 us (7%)
  local copies, waits for them, and re-layouts  18 us (1%)
    ppermute x127, waiting for transfers between devices, passed_along(): lax.ppermute(array, axis, [(i, (i + by) % count) for i in range(count)])  1130 us
    all_gather x1, waiting for transfers between devices, per_device(): lax.all_gather(coefficients, 'blk', axis=0, tiled=True)  223 us
    dot_general x128, matrix products, tile_product(): jnp.einsum('pri,psi->rs', local_rows, other, preferred_element_type=jnp.f...  103 us
    reduce_scatter x1, waiting for transfers between devices, per_device(): lax.psum_scatter(exchange_rows, 'aux', scatter_dimension=1, tiled=True)  54.4 us
  transfers between devices with their start and end apart: 130, of which 130 were waited for; matrix products, arithmetic and copies ran while one was open for 0% of the time, Pallas kernels for 0%

commit v1 on v0

v1 whole, which is shorter than its diff:
```python
import jax
import jax.numpy as jnp
from jax import lax
from jax.experimental import pallas as pl
from jax.experimental.pallas import tpu as pltpu
from jax.sharding import Mesh, PartitionSpec as P

AXES = ("yh", "z", "yl", "x", "c")
SIZES = (2, 8, 2, 4, 2)
Y = ("yh", "yl")
ROWS, OCC, AUX, BASIS = 80, 256, 4, 10240
DEPTH = AUX * OCC
RING4 = (0, 3, 1, 2)
RING8 = (0, 7, 1, 6, 2, 5, 3, 4)
MIB = 1 << 20
VMEM = pl.BlockSpec(memory_space=pltpu.VMEM)
SMEM = pl.BlockSpec(memory_space=pltpu.SMEM)


def shift(value, axis, by):
    count = lax.axis_size(axis)
    return lax.ppermute(value, axis, [(i, (i + by) % count) for i in range(count)])


def swap(value):
    return shift(value, "c", 1)


def together(*values):
    return lax.optimization_barrier(values)


def call(kernel, outs, ins, mib, scratch=(), flops=0, moved=1):
    shapes = [jax.ShapeDtypeStruct(shape, jnp.bfloat16) for shape in outs]
    return pl.pallas_call(
        kernel,
        out_shape=shapes,
        in_specs=[spec for spec, _ in ins],
        out_specs=[VMEM] * len(shapes),
        scratch_shapes=list(scratch),
        compiler_params=pltpu.CompilerParams(vmem_limit_bytes=mib * MIB),
        cost_estimate=pl.CostEstimate(flops=flops, bytes_accessed=moved, transcendentals=0),
    )(*[value for _, value in ins])


def everywhere(value, axes):
    count = lax.axis_size(axes)
    copies = jnp.broadcast_to(value[None], (count,) + value.shape)
    return lax.all_to_all(copies, axes, split_axis=0, concat_axis=0, tiled=True)


def cut_kernel(first, second, *refs):
    low, high = refs[-2:]
    half = low.shape[0]
    low[...] = first[:half]
    high[...] = second[half:]


def cut(first, second, *also):
    half = (first.shape[0] // 2,) + first.shape[1:]
    return call(cut_kernel, [half, half], [(VMEM, v) for v in (first, second, *also)], 4)


def transform_kernel(where, integrals, *refs):
    pieces, (out, coefs) = refs[:-2], refs[-2:]
    yl, x, c = where[1], where[3], where[4]

    def keep(ref, core, other_y, along_x, first):
        low = 1 - yl if other_y else yl
        at_x = lax.rem(x + along_x + 4, 4)
        for i in range(ref.shape[0]):
            coefs[first + i, (low * 4 + at_x) * 2 + core] = ref[i]

    count = len(pieces) // 2
    for other in range(2):
        core = 1 - c if other else c
        near, left, right, far0, far1, ynear0, ynear1, yleft, yright, yfar0, yfar1 = pieces[other * count:(other + 1) * count]
        for ref, other_y, at_x, first in (
            (near, 0, 0, 0), (left, 0, -1, 0), (right, 0, 1, 0), (far0, 0, 2, 0), (far1, 0, 2, 4),
            (ynear0, 1, 0, 0), (ynear1, 1, 0, 4), (yleft, 1, -1, 0), (yright, 1, 1, 0), (yfar0, 1, 2, 0), (yfar1, 1, 2, 4),
        ):
            keep(ref, core, other_y, at_x, first)

    total = jnp.zeros((AUX * ROWS, OCC), jnp.float32)
    for z in range(8):
        chunk = coefs[z].reshape(1280, OCC)
        total += jnp.dot(integrals[:, z * 1280:(z + 1) * 1280], chunk, preferred_element_type=jnp.float32)
    half = total.astype(jnp.bfloat16)
    for p in range(AUX):
        out[:, p * OCC:(p + 1) * OCC] = half[p * ROWS:(p + 1) * ROWS]


def transform(where, flat, pieces):
    return call(
        transform_kernel,
        [(ROWS, DEPTH)],
        [(SMEM, where), (VMEM, flat)] + [(VMEM, p) for p in pieces],
        16,
        [pltpu.VMEM((8, 16, ROWS, OCC), jnp.bfloat16)],
        2 * 320 * BASIS * OCC, 12 * MIB,
    )[0]


def held_kernel(where, unit, moved, out):
    home = where[0] == where[2] // 4

    @pl.when(home)
    def _():
        out[...] = unit[...]

    @pl.when(jnp.logical_not(home))
    def _():
        out[...] = moved[...]


def stack_kernel(*refs):
    for i, ref in enumerate(refs[:-1]):
        refs[-1][i] = ref[...]


def stack(*values):
    return call(stack_kernel, [(len(values),) + values[0].shape], [(VMEM, v) for v in values], 4)[0]


def product_kernel(where, near, left, right, far0, far1, *refs):
    cols, (out, lefts, rights) = refs[:16], refs[16:]
    yh, yl, z, x, c = (where[i] for i in range(5))
    for ref, along_x, first in ((near, 0, 0), (left, 3, 0), (right, 1, 0), (far0, 2, 0), (far1, 2, 2)):
        at_x = lax.rem(x + along_x, 4)
        for i in range(ref.shape[0]):
            at_y = lax.rem(yh * 2 + yl + RING4[first + i], 4)
            lefts[at_y // 2, (at_y % 2) * 4 + at_x] = ref[i]
    for other in range(2):
        core = 1 - c if other else c
        for ref, along in zip(cols[other * 8:other * 8 + 8], RING8):
            at_z = lax.rem(z + along, 8)
            side = at_z // 4
            q = jnp.where(side == yh, at_z % 4, 3 - at_z % 4)
            rights[side, q * 2 + core] = ref[...]
    total = None
    for side in range(2):
        part = lax.dot_general(
            lefts[side].reshape(640, DEPTH), rights[side].reshape(640, DEPTH),
            (((1,), (1,)), ((), ())), preferred_element_type=jnp.float32,
        )
        total = part if total is None else total + part
    out[...] = total.astype(jnp.bfloat16).reshape(8, ROWS, 640)


def product(where, rows, cols):
    return call(
        product_kernel,
        [(8, ROWS, 640)],
        [(SMEM, where)] + [(VMEM, v) for v in rows + cols],
        16,
        [pltpu.VMEM((2, 8, ROWS, DEPTH), jnp.bfloat16)] * 2,
        2 * 640 * 640 * 2 * DEPTH, 6 * MIB,
    )[0]


def spread_kernel(pieces, out):
    for q in range(4):
        for s in range(8):
            at = q * 1280 + s * 160
            out[:, at:at + 160] = pieces[s, :, q * 160:(q + 1) * 160].astype(jnp.float32)


def spread(pieces):
    return pl.pallas_call(
        spread_kernel,
        out_shape=jax.ShapeDtypeStruct((ROWS, 5120), jnp.float32),
        in_specs=[VMEM],
        out_specs=VMEM,
        compiler_params=pltpu.CompilerParams(vmem_limit_bytes=8 * MIB),
        cost_estimate=pl.CostEstimate(flops=0, bytes_accessed=4 * MIB, transcendentals=0),
    )(pieces)


def gather_coefficients(own, flat):
    near = everywhere(own, "z")
    low, high = cut(near, near, flat)
    left, right = shift(near, "x", 1), shift(near, "x", -1)
    ynear = shift(low, Y, 1), shift(high, Y, -1)
    left, right = together(left, right)
    far = cut(left, right)
    far = shift(far[0], "x", 1), shift(far[1], "x", -1)
    yleft, yright = shift(left, Y, 1), shift(right, Y, -1)
    *far, yleft, yright = together(*far, yleft, yright)
    yfar = together(shift(far[0], Y, 1), shift(far[1], Y, -1))
    return [near, left, right, *far, *ynear, yleft, yright, *yfar]


def per_device(integrals, coefficients):
    where = jnp.stack([lax.axis_index(a) for a in ("yh", "yl", "z", "x", "c")]).astype(jnp.int32)
    where, coefficients = together(where, coefficients)
    flat = integrals.reshape(AUX * ROWS, BASIS)

    pieces = gather_coefficients(coefficients, flat)
    pieces += [swap(p) for p in pieces]
    unit = transform(where, flat, pieces)

    moves = []
    for zi in range(8):
        home = zi // 4
        moves.append(((1 - home) * 8 + zi, home * 8 + 7 - zi))
    moved = lax.ppermute(unit, ("yh", "z"), moves)
    at_y = stack(unit, shift(unit, Y, 1), shift(unit, Y, -1), shift(unit, Y, 2))
    held = call(held_kernel, [unit.shape], [(SMEM, where), (VMEM, unit), (VMEM, moved)], 4)[0]

    up, down = shift(held, "z", 1), shift(held, "z", -1)
    up, down, at_y = together(up, down, at_y)
    left, right = shift(at_y, "x", 1), shift(at_y, "x", -1)
    up2, down2 = shift(up, "z", 1), shift(down, "z", -1)
    up3, down3 = shift(up2, "z", 1), shift(down2, "z", -1)
    up3, down3, left, right = together(up3, down3, left, right)
    far = cut(left, right)
    far = [shift(far[0], "x", 1), shift(far[1], "x", -1)]
    up4 = shift(up3, "z", 1)
    up4, *far = together(up4, *far)
    cols = [held, up, down, up2, down2, up3, down3, up4]
    cols += [swap(v) for v in cols]

    block = product(where, [at_y, left, right, *far], cols)
    return spread(lax.all_to_all(block, ("yl", "x"), split_axis=0, concat_axis=0, tiled=True))


def solution(mesh):
    fine = Mesh(mesh.devices.reshape(SIZES), AXES)
    blk = ("z", "yl", "x", "c")
    return jax.shard_map(
        per_device,
        mesh=fine,
        in_specs=(P("yh", blk, None), P(blk, None)),
        out_specs=P(blk, "yh"),
        check_vma=False,
    )
```

time: 1560 us -> 134 us (0.09)
  waiting for transfers between devices: 1410 us -> 20.7 us
  matrix products: 109 us -> 0 us
  starting transfers between devices: 11 us -> 64 us
  blocking collectives: 0 us -> 36.5 us
    ppermute x127 -> x44, waiting for transfers between devices: 1130 us -> 20.7 us  [the longest x43 20.7 us: shift(): lax.ppermute(value, axis, [(i, (i + by) % count) for i in range(count)])]
    all_gather x1 -> x0, waiting for transfers between devices: 223 us -> none  [per_device(): lax.all_gather(coefficients, 'blk', axis=0, tiled=True)]
    dot_general x129 -> x0, matrix products: 109 us -> none  [the longest x128 103 us: tile_product(): jnp.einsum('pri,psi->rs', local_rows, other, preferred_element_type=jnp.f...]
    ppermute x127 -> x44, starting transfers between devices: 7 us -> 64 us  [the longest x43 63.4 us: shift(): lax.ppermute(value, axis, [(i, (i + by) % count) for i in range(count)])]
    reduce_scatter x1 -> x0, waiting for transfers between devices: 54.4 us -> none  [per_device(): lax.psum_scatter(exchange_rows, 'aux', scatter_dimension=1, tiled=True)]
    all_to_all x0 -> x2, blocking collectives: none -> 36.5 us  [the longest x1 20.5 us: everywhere(): return lax.all_to_all(copies, axes, split_axis=0, concat_axis=0, tiled=True)]
  transfers between devices with their start and end apart: 130 -> 44, of which waited for: 130 -> 13; matrix products, arithmetic and copies ran while one was open for 0% -> 0% of each run, Pallas kernels for 0% -> 0%
where the time goes in v1:
time: 134 us; the launch traced here: 133 us
  starting transfers between devices  64 us (48%)
  blocking collectives  36.5 us (27%)
  waiting for transfers between devices  20.7 us (15%)
  Pallas kernels  8.11 us (6%)
  local copies, waits for them, and re-layouts  3.75 us (3%)
    ppermute x43, starting transfers between devices, shift(): lax.ppermute(value, axis, [(i, (i + by) % count) for i in range(count)])  63.4 us
    ppermute x43, waiting for transfers between devices, shift(): lax.ppermute(value, axis, [(i, (i + by) % count) for i in range(count)])  20.7 us
    all_to_all x1, blocking collectives, everywhere(): return lax.all_to_all(copies, axes, split_axis=0, concat_axis=0, tiled=True)  20.5 us
    all_to_all x1, blocking collectives, per_device(): lax.all_to_all(block, ('yl', 'x'), split_axis=0, concat_axis=0, tiled=True)  16 us
    pallas_call x7, Pallas kernels, call(): pl.pallas_call(kernel, out_shape=shapes, in_specs=[spec for spec, _ in in...  6.61 us
    unnamed x4, local copies, waits for them, and re-layouts  2.86 us
  transfers between devices with their start and end apart: 44, of which 13 were waited for; matrix products, arithmetic and copies ran while one was open for 0% of the time, Pallas kernels for 0%

profile of v1, /device:TPU:1, one launch (start us, length us, event | category | flops | bytes accessed | tf_op | source)
XLA Modules:
  0.0 133.3 jit_solution(9077577970136621557)
XLA Ops:
  0.9 20.5 %all_to_all.10.first.second.refs_0_ = bf16[8,80,256]{2,1,0:T(8,128)(2,1)S(1)} all-to-all(bf16[8,80,256]{2,1,0:T(8,128)(2,1)S(1)} %broadcast_in_dim.2), channel_id=1, replica_groups=mesh['yh'=2,'z'=8,'yl'=2,'x'=4,'c'=2] {'z'}, dimensions={0} | all-to-all | bytes 655360 | tf_op jit(solution)/shard_map/all_to_all | solution.py:49
  21.4 2.5 %collective-permute-start.1 = (bf16[8,80,256]{2,1,0:T(8,128)(2,1)S(1)}, bf16[8,80,256]{2,1,0:T(8,128)(2,1)S(1)}, u32[]{:S(2)}, u32[]{:S(2)}) collective-permute-start(bf16[8,80,256]{2,1,0:T(8,128)(2,1)S(1)} %all_to_all.10.first.second.refs_0_), channel_id=1, source_target_pairs={{0,6},{2,0},{4,2},{6,4},{1,7},{3,1},{5,3},{7,5},{8,14},{10,8},{12,... | collective-permute-start | bytes 983048 | tf_op jit(solution)/shard_map/ppermute | solution.py:22
  23.9 2.9 %copy-done = bf16[4,80,10240]{2,1,0:T(8,128)(2,1)S(1)} copy-done((bf16[4,80,10240]{2,1,0:T(8,128)(2,1)S(1)}, bf16[4,80,10240]{2,1,0:T(8,128)(2,1)}, u32[]{:S(2)}) %copy-start) | copy-done | bytes 6553624
  26.7 1.4 %collective-permute-start.6 = (bf16[4,80,256]{2,1,0:T(8,128)(2,1)S(1)}, bf16[4,80,256]{2,1,0:T(8,128)(2,1)S(1)}, u32[]{:S(2)}, u32[]{:S(2)}) collective-permute-start(bf16[4,80,256]{2,1,0:T(8,128)(2,1)S(1)} %get-tuple-element.39), channel_id=1, source_target_pairs={{0,8},{8,128},{128,136},{136,0},{1,9},{9,129},{129,137},{137,1},{2... | collective-permute-start | bytes 491528 | tf_op jit(solution)/shard_map/ppermute | solution.py:22
  28.1 1.5 %collective-permute-start.7 = (bf16[4,80,256]{2,1,0:T(8,128)(2,1)S(1)}, bf16[4,80,256]{2,1,0:T(8,128)(2,1)S(1)}, u32[]{:S(2)}, u32[]{:S(2)}) collective-permute-start(bf16[4,80,256]{2,1,0:T(8,128)(2,1)S(1)} %get-tuple-element.40), channel_id=1, source_target_pairs={{0,136},{8,0},{128,8},{136,128},{1,137},{9,1},{129,9},{137,129},{2... | collective-permute-start | bytes 491528 | tf_op jit(solution)/shard_map/ppermute | solution.py:22
  29.6 1.8 %collective-permute-done.first.refs_1_ = bf16[8,80,256]{2,1,0:T(8,128)(2,1)S(1)} collective-permute-done((bf16[8,80,256]{2,1,0:T(8,128)(2,1)S(1)}, bf16[8,80,256]{2,1,0:T(8,128)(2,1)S(1)}, u32[]{:S(2)}, u32[]{:S(2)}) %collective-permute-start) | collective-permute-done | bytes 327712 | tf_op jit(solution)/shard_map/ppermute | solution.py:22
  31.4 1.3 collective-permute-start.4
  32.7 1.4 %collective-permute-start.5 = (bf16[8,80,256]{2,1,0:T(8,128)(2,1)S(1)}, bf16[8,80,256]{2,1,0:T(8,128)(2,1)S(1)}, u32[]{:S(2)}, u32[]{:S(2)}) collective-permute-start(bf16[8,80,256]{2,1,0:T(8,128)(2,1)S(1)} %collective-permute-done.1.second.refs_2_), channel_id=1, source_target_pairs={{0,136},{8,0},{128,8},{136,128},{1,137},{9,1},{129,9},{137,129},{2... | collective-permute-start | bytes 983048 | tf_op jit(solution)/shard_map/ppermute | solution.py:22
  34.3 2.7 %collective-permute-start.3 = (bf16[4,80,256]{2,1,0:T(8,128)(2,1)S(1)}, bf16[4,80,256]{2,1,0:T(8,128)(2,1)S(1)}, u32[]{:S(2)}, u32[]{:S(2)}) collective-permute-start(bf16[4,80,256]{2,1,0:T(8,128)(2,1)S(1)} %get-tuple-element.36), channel_id=1, source_target_pairs={{0,6},{2,0},{4,2},{6,4},{1,7},{3,1},{5,3},{7,5},{8,14},{10,8},{12,... | collective-permute-start | bytes 491528 | tf_op jit(solution)/shard_map/ppermute | solution.py:22
  36.9 4.8 %collective-permute-start.15 = (bf16[4,80,256]{2,1,0:T(8,128)(2,1)S(1)}, bf16[4,80,256]{2,1,0:T(8,128)(2,1)S(1)}, u32[]{:S(2)}, u32[]{:S(2)}) collective-permute-start(bf16[4,80,256]{2,1,0:T(8,128)(2,1)S(1)} %collective-permute-done.6.refs_5_), channel_id=1, source_target_pairs={{0,1},{1,0},{2,3},{3,2},{4,5},{5,4},{6,7},{7,6},{8,9},{9,8},{10,11... | collective-permute-start | bytes 491528 | tf_op jit(solution)/shard_map/ppermute | solution.py:22
  41.8 3.3 %collective-permute-start.10 = (bf16[8,80,256]{2,1,0:T(8,128)(2,1)S(1)}, bf16[8,80,256]{2,1,0:T(8,128)(2,1)S(1)}, u32[]{:S(2)}, u32[]{:S(2)}) collective-permute-start(bf16[8,80,256]{2,1,0:T(8,128)(2,1)S(1)} %all_to_all.10.first.second.refs_0_), channel_id=1, source_target_pairs={{0,1},{1,0},{2,3},{3,2},{4,5},{5,4},{6,7},{7,6},{8,9},{9,8},{10,11... | collective-permute-start | bytes 983048 | tf_op jit(solution)/shard_map/ppermute | solution.py:22
  46.5 1.8 %collective-permute-start.9 = (bf16[4,80,256]{2,1,0:T(8,128)(2,1)S(1)}, bf16[4,80,256]{2,1,0:T(8,128)(2,1)S(1)}, u32[]{:S(2)}, u32[]{:S(2)}) collective-permute-start(bf16[4,80,256]{2,1,0:T(8,128)(2,1)S(1)} %collective-permute-done.3.refs_4_), channel_id=1, source_target_pairs={{0,136},{8,0},{128,8},{136,128},{1,137},{9,1},{129,9},{137,129},{2... | collective-permute-start | bytes 491528 | tf_op jit(solution)/shard_map/ppermute | solution.py:22
  49.3 2.9 %collective-permute-done.8.refs_9_ = bf16[4,80,256]{2,1,0:T(8,128)(2,1)S(1)} collective-permute-done((bf16[4,80,256]{2,1,0:T(8,128)(2,1)S(1)}, bf16[4,80,256]{2,1,0:T(8,128)(2,1)S(1)}, u32[]{:S(2)}, u32[]{:S(2)}) %collective-permute-start.8) | collective-permute-done | bytes 163872 | tf_op jit(solution)/shard_map/ppermute | solution.py:22
  52.2 1.3 collective-permute-start.17
  55.9 2.8 %shard_map.30.unit.refs_0_ = bf16[80,1024]{1,0:T(8,128)(2,1)S(1)} custom-call(s32[5]{0:T(128)S(1)} %stack.23.where, bf16[320,10240]{1,0:T(8,128)(2,1)S(1)} %bitcast.7, bf16[8,80,256]{2,1,0:T(8,128)(2,1)S(1)} %all_to_all.10.first.second.refs_0_, bf16[8,80,256]{2,1,0:T(8,128)(2,1)S(1)} %collective-permute-done.first.refs_1_, ...), custom_call_target="tpu_custom_call" | custom-call | flops 1677721600 | bytes 12582912 | tf_op jit(solution)/shard_map/pallas_call | solution.py:35
  59.4 3.5 %collective-permute-start.26 = (bf16[80,1024]{1,0:T(8,128)(2,1)S(1)}, bf16[80,1024]{1,0:T(8,128)(2,1)S(1)}, u32[]{:S(2)}, u32[]{:S(2)}) collective-permute-start(bf16[80,1024]{1,0:T(8,128)(2,1)S(1)} %shard_map.30.unit.refs_0_), channel_id=1, source_target_pairs={{0,128},{8,136},{128,0},{136,8},{1,129},{9,137},{129,1},{137,9},{2... | collective-permute-start | bytes 491528 | tf_op jit(solution)/shard_map/ppermute | solution.py:22
  63.0 1.4 %collective-permute-start.24 = (bf16[80,1024]{1,0:T(8,128)(2,1)S(1)}, bf16[80,1024]{1,0:T(8,128)(2,1)S(1)}, u32[]{:S(2)}, u32[]{:S(2)}) collective-permute-start(bf16[80,1024]{1,0:T(8,128)(2,1)S(1)} %shard_map.30.unit.refs_0_), channel_id=1, source_target_pairs={{0,8},{8,128},{128,136},{136,0},{1,9},{9,129},{129,137},{137,1},{2... | collective-permute-start | bytes 491528 | tf_op jit(solution)/shard_map/ppermute | solution.py:22
  65.0 6.5 %collective-permute-start.23 = (bf16[80,1024]{1,0:T(8,128)(2,1)S(1)}, bf16[80,1024]{1,0:T(8,128)(2,1)S(1)}, u32[]{:S(2)}, u32[]{:S(2)}) collective-permute-start(bf16[80,1024]{1,0:T(8,128)(2,1)S(1)} %shard_map.31.refs_0_), channel_id=1, source_target_pairs={{0,112},{16,0},{32,16},{48,32},{64,48},{80,64},{96,80},{112,96},{1... | collective-permute-start | bytes 491528 | tf_op jit(solution)/shard_map/ppermute | solution.py:22
  71.4 3.1 %collective-permute-done.25.refs_2_ = bf16[80,1024]{1,0:T(8,128)(2,1)S(1)} collective-permute-done((bf16[80,1024]{1,0:T(8,128)(2,1)S(1)}, bf16[80,1024]{1,0:T(8,128)(2,1)S(1)}, u32[]{:S(2)}, u32[]{:S(2)}) %collective-permute-start.25) | collective-permute-done | bytes 163872 | tf_op jit(solution)/shard_map/ppermute | solution.py:22
  74.6 2.3 %collective-permute-done.22.refs_1_ = bf16[80,1024]{1,0:T(8,128)(2,1)S(1)} collective-permute-done((bf16[80,1024]{1,0:T(8,128)(2,1)S(1)}, bf16[80,1024]{1,0:T(8,128)(2,1)S(1)}, u32[]{:S(2)}, u32[]{:S(2)}) %collective-permute-start.22) | collective-permute-done | bytes 163872 | tf_op jit(solution)/shard_map/ppermute | solution.py:22
  76.9 2.9 %collective-permute-start.32 = (bf16[4,80,1024]{2,1,0:T(8,128)(2,1)S(1)}, bf16[4,80,1024]{2,1,0:T(8,128)(2,1)S(1)}, u32[]{:S(2)}, u32[]{:S(2)}) collective-permute-start(bf16[4,80,1024]{2,1,0:T(8,128)(2,1)S(1)} %shard_map.32.near), channel_id=1, source_target_pairs={{0,6},{2,0},{4,2},{6,4},{1,7},{3,1},{5,3},{7,5},{8,14},{10,8},{12,... | collective-permute-start | bytes 1966088 | tf_op jit(solution)/shard_map/ppermute | solution.py:22
  79.8 2.7 %collective-permute-start.29 = (bf16[80,1024]{1,0:T(8,128)(2,1)S(1)}, bf16[80,1024]{1,0:T(8,128)(2,1)S(1)}, u32[]{:S(2)}, u32[]{:S(2)}) collective-permute-start(bf16[80,1024]{1,0:T(8,128)(2,1)S(1)} %collective-permute-done.23.refs_2_), channel_id=1, source_target_pairs={{0,112},{16,0},{32,16},{48,32},{64,48},{80,64},{96,80},{112,96},{1... | collective-permute-start | bytes 491528 | tf_op jit(solution)/shard_map/ppermute | solution.py:22
  82.4 2.7 %collective-permute-done.27.refs_3_ = bf16[80,1024]{1,0:T(8,128)(2,1)S(1)} collective-permute-done((bf16[80,1024]{1,0:T(8,128)(2,1)S(1)}, bf16[80,1024]{1,0:T(8,128)(2,1)S(1)}, u32[]{:S(2)}, u32[]{:S(2)}) %collective-permute-start.27) | collective-permute-done | bytes 163872 | tf_op jit(solution)/shard_map/ppermute | solution.py:22
  85.2 2.7 %collective-permute-start.30 = (bf16[80,1024]{1,0:T(8,128)(2,1)S(1)}, bf16[80,1024]{1,0:T(8,128)(2,1)S(1)}, u32[]{:S(2)}, u32[]{:S(2)}) collective-permute-start(bf16[80,1024]{1,0:T(8,128)(2,1)S(1)} %collective-permute-done.29.refs_4_), channel_id=1, source_target_pairs={{0,112},{16,0},{32,16},{48,32},{64,48},{80,64},{96,80},{112,96},{1... | collective-permute-start | bytes 491528 | tf_op jit(solution)/shard_map/ppermute | solution.py:22
  87.8 4.7 %collective-permute-done.28.refs_5_ = bf16[80,1024]{1,0:T(8,128)(2,1)S(1)} collective-permute-done((bf16[80,1024]{1,0:T(8,128)(2,1)S(1)}, bf16[80,1024]{1,0:T(8,128)(2,1)S(1)}, u32[]{:S(2)}, u32[]{:S(2)}) %collective-permute-start.28) | collective-permute-done | bytes 163872 | tf_op jit(solution)/shard_map/ppermute | solution.py:22
  92.9 2.7 %collective-permute-start.35 = (bf16[2,80,1024]{2,1,0:T(8,128)(2,1)S(1)}, bf16[2,80,1024]{2,1,0:T(8,128)(2,1)S(1)}, u32[]{:S(2)}, u32[]{:S(2)}) collective-permute-start(bf16[2,80,1024]{2,1,0:T(8,128)(2,1)S(1)} %get-tuple-element.52), channel_id=1, source_target_pairs={{0,6},{2,0},{4,2},{6,4},{1,7},{3,1},{5,3},{7,5},{8,14},{10,8},{12,... | collective-permute-start | bytes 983048 | tf_op jit(solution)/shard_map/ppermute | solution.py:22
  95.6 1.3 collective-permute-start.33
  96.9 6.7 %collective-permute-start.36 = (bf16[80,1024]{1,0:T(8,128)(2,1)S(1)}, bf16[80,1024]{1,0:T(8,128)(2,1)S(1)}, u32[]{:S(2)}, u32[]{:S(2)}) collective-permute-start(bf16[80,1024]{1,0:T(8,128)(2,1)S(1)} %shard_map.31.refs_0_), channel_id=1, source_target_pairs={{0,1},{1,0},{2,3},{3,2},{4,5},{5,4},{6,7},{7,6},{8,9},{9,8},{10,11... | collective-permute-start | bytes 491528 | tf_op jit(solution)/shard_map/ppermute | solution.py:22
  103.6 6.5 %collective-permute-start.38 = (bf16[80,1024]{1,0:T(8,128)(2,1)S(1)}, bf16[80,1024]{1,0:T(8,128)(2,1)S(1)}, u32[]{:S(2)}, u32[]{:S(2)}) collective-permute-start(bf16[80,1024]{1,0:T(8,128)(2,1)S(1)} %collective-permute-done.23.refs_2_), channel_id=1, source_target_pairs={{0,1},{1,0},{2,3},{3,2},{4,5},{5,4},{6,7},{7,6},{8,9},{9,8},{10,11... | collective-permute-start | bytes 491528 | tf_op jit(solution)/shard_map/ppermute | solution.py:22
  112.6 3.1 %shard_map.34 = bf16[8,80,640]{2,1,0:T(8,128)(2,1)S(1)} custom-call(s32[5]{0:T(128)S(1)} %stack.23.where, bf16[4,80,1024]{2,1,0:T(8,128)(2,1)S(1)} %shard_map.32.near, bf16[4,80,1024]{2,1,0:T(8,128)(2,1)S(1)} %collective-permute-done.31.first.left, bf16[4,80,1024]{2,1,0:T(8,128)(2,1)S(1)} %collective-permute-done.32.second.right, ...), custom_call_target="tpu_custom_call" | custom-call | flops 1677721600 | bytes 6291456 | tf_op jit(solution)/shard_map/pallas_call | solution.py:35
  115.7 16.0 %all_to_all.11.pieces = bf16[8,80,640]{2,1,0:T(8,128)(2,1)S(1)} all-to-all(bf16[8,80,640]{2,1,0:T(8,128)(2,1)S(1)} %shard_map.34), channel_id=1, replica_groups=mesh['yh'=2,'z'=8,'yl'=2,'x'=4,'c'=2] {'yl','x'}, dimensions={0} | all-to-all | bytes 1638400 | tf_op jit(solution)/shard_map/all_to_all | solution.py:224
  131.8 1.5 %shard_map.35 = f32[80,5120]{1,0:T(8,128)} custom-call(bf16[8,80,640]{2,1,0:T(8,128)(2,1)S(1)} %all_to_all.11.pieces), custom_call_target="tpu_custom_call" | custom-call | bytes 4194304 | tf_op jit(solution)/shard_map/pallas_call | solution.py:169
  (72 shorter events, 10.1 us)
Async XLA Ops:
  21.4 8.3 %collective-permute-start.1 = (bf16[8,80,256]{2,1,0:T(8,128)(2,1)S(1)}, bf16[8,80,256]{2,1,0:T(8,128)(2,1)S(1)}, u32[]{:S(2)}, u32[]{:S(2)}) collective-permute-start(bf16[8,80,256]{2,1,0:T(8,128)(2,1)S(1)} %all_to_all.10.first.second.refs_0_), channel_id=1, source_target_pairs={{0,6},{2,0},{4,2},{6,4},{1,7},{3,1},{5,3},{7,5},{8,14},{10,8},{12,... | collective-permute-start | bytes 983048 | tf_op jit(solution)/shard_map/ppermute | solution.py:22
  23.9 7.6 %collective-permute-start = (bf16[8,80,256]{2,1,0:T(8,128)(2,1)S(1)}, bf16[8,80,256]{2,1,0:T(8,128)(2,1)S(1)}, u32[]{:S(2)}, u32[]{:S(2)}) collective-permute-start(bf16[8,80,256]{2,1,0:T(8,128)(2,1)S(1)} %all_to_all.10.first.second.refs_0_), channel_id=1, source_target_pairs={{0,2},{2,4},{4,6},{6,0},{1,3},{3,5},{5,7},{7,1},{8,10},{10,12},{12... | collective-permute-start | bytes 983048 | tf_op jit(solution)/shard_map/ppermute | solution.py:22
  26.7 7.5 %collective-permute-start.6 = (bf16[4,80,256]{2,1,0:T(8,128)(2,1)S(1)}, bf16[4,80,256]{2,1,0:T(8,128)(2,1)S(1)}, u32[]{:S(2)}, u32[]{:S(2)}) collective-permute-start(bf16[4,80,256]{2,1,0:T(8,128)(2,1)S(1)} %get-tuple-element.39), channel_id=1, source_target_pairs={{0,8},{8,128},{128,136},{136,0},{1,9},{9,129},{129,137},{137,1},{2... | collective-permute-start | bytes 491528 | tf_op jit(solution)/shard_map/ppermute | solution.py:22
  28.1 8.8 %collective-permute-start.7 = (bf16[4,80,256]{2,1,0:T(8,128)(2,1)S(1)}, bf16[4,80,256]{2,1,0:T(8,128)(2,1)S(1)}, u32[]{:S(2)}, u32[]{:S(2)}) collective-permute-start(bf16[4,80,256]{2,1,0:T(8,128)(2,1)S(1)} %get-tuple-element.40), channel_id=1, source_target_pairs={{0,136},{8,0},{128,8},{136,128},{1,137},{9,1},{129,9},{137,129},{2... | collective-permute-start | bytes 491528 | tf_op jit(solution)/shard_map/ppermute | solution.py:22
  31.4 13.7 %collective-permute-start.4 = (bf16[8,80,256]{2,1,0:T(8,128)(2,1)S(1)}, bf16[8,80,256]{2,1,0:T(8,128)(2,1)S(1)}, u32[]{:S(2)}, u32[]{:S(2)}) collective-permute-start(bf16[8,80,256]{2,1,0:T(8,128)(2,1)S(1)} %collective-permute-done.first.refs_1_), channel_id=1, source_target_pairs={{0,8},{8,128},{128,136},{136,0},{1,9},{9,129},{129,137},{137,1},{2... | collective-permute-start | bytes 983048 | tf_op jit(solution)/shard_map/ppermute | solution.py:22
  32.7 12.9 %collective-permute-start.5 = (bf16[8,80,256]{2,1,0:T(8,128)(2,1)S(1)}, bf16[8,80,256]{2,1,0:T(8,128)(2,1)S(1)}, u32[]{:S(2)}, u32[]{:S(2)}) collective-permute-start(bf16[8,80,256]{2,1,0:T(8,128)(2,1)S(1)} %collective-permute-done.1.second.refs_2_), channel_id=1, source_target_pairs={{0,136},{8,0},{128,8},{136,128},{1,137},{9,1},{129,9},{137,129},{2... | collective-permute-start | bytes 983048 | tf_op jit(solution)/shard_map/ppermute | solution.py:22
  34.2 7.6 %collective-permute-start.2 = (bf16[4,80,256]{2,1,0:T(8,128)(2,1)S(1)}, bf16[4,80,256]{2,1,0:T(8,128)(2,1)S(1)}, u32[]{:S(2)}, u32[]{:S(2)}) collective-permute-start(bf16[4,80,256]{2,1,0:T(8,128)(2,1)S(1)} %get-tuple-element.35), channel_id=1, source_target_pairs={{0,2},{2,4},{4,6},{6,0},{1,3},{3,5},{5,7},{7,1},{8,10},{10,12},{12... | collective-permute-start | bytes 491528 | tf_op jit(solution)/shard_map/ppermute | solution.py:22
  34.3 10.8 %collective-permute-start.3 = (bf16[4,80,256]{2,1,0:T(8,128)(2,1)S(1)}, bf16[4,80,256]{2,1,0:T(8,128)(2,1)S(1)}, u32[]{:S(2)}, u32[]{:S(2)}) collective-permute-start(bf16[4,80,256]{2,1,0:T(8,128)(2,1)S(1)} %get-tuple-element.36), channel_id=1, source_target_pairs={{0,6},{2,0},{4,2},{6,4},{1,7},{3,1},{5,3},{7,5},{8,14},{10,8},{12,... | collective-permute-start | bytes 491528 | tf_op jit(solution)/shard_map/ppermute | solution.py:22
  36.9 8.7 %collective-permute-start.15 = (bf16[4,80,256]{2,1,0:T(8,128)(2,1)S(1)}, bf16[4,80,256]{2,1,0:T(8,128)(2,1)S(1)}, u32[]{:S(2)}, u32[]{:S(2)}) collective-permute-start(bf16[4,80,256]{2,1,0:T(8,128)(2,1)S(1)} %collective-permute-done.6.refs_5_), channel_id=1, source_target_pairs={{0,1},{1,0},{2,3},{3,2},{4,5},{5,4},{6,7},{7,6},{8,9},{9,8},{10,11... | collective-permute-start | bytes 491528 | tf_op jit(solution)/shard_map/ppermute | solution.py:22
  41.8 6.6 %collective-permute-start.10 = (bf16[8,80,256]{2,1,0:T(8,128)(2,1)S(1)}, bf16[8,80,256]{2,1,0:T(8,128)(2,1)S(1)}, u32[]{:S(2)}, u32[]{:S(2)}) collective-permute-start(bf16[8,80,256]{2,1,0:T(8,128)(2,1)S(1)} %all_to_all.10.first.second.refs_0_), channel_id=1, source_target_pairs={{0,1},{1,0},{2,3},{3,2},{4,5},{5,4},{6,7},{7,6},{8,9},{9,8},{10,11... | collective-permute-start | bytes 983048 | tf_op jit(solution)/shard_map/ppermute | solution.py:22
  45.1 8.4 %collective-permute-start.11 = (bf16[8,80,256]{2,1,0:T(8,128)(2,1)S(1)}, bf16[8,80,256]{2,1,0:T(8,128)(2,1)S(1)}, u32[]{:S(2)}, u32[]{:S(2)}) collective-permute-start(bf16[8,80,256]{2,1,0:T(8,128)(2,1)S(1)} %collective-permute-done.first.refs_1_), channel_id=1, source_target_pairs={{0,1},{1,0},{2,3},{3,2},{4,5},{5,4},{6,7},{7,6},{8,9},{9,8},{10,11... | collective-permute-start | bytes 983048 | tf_op jit(solution)/shard_map/ppermute | solution.py:22
  45.6 8.4 %collective-permute-start.12 = (bf16[8,80,256]{2,1,0:T(8,128)(2,1)S(1)}, bf16[8,80,256]{2,1,0:T(8,128)(2,1)S(1)}, u32[]{:S(2)}, u32[]{:S(2)}) collective-permute-start(bf16[8,80,256]{2,1,0:T(8,128)(2,1)S(1)} %collective-permute-done.1.second.refs_2_), channel_id=1, source_target_pairs={{0,1},{1,0},{2,3},{3,2},{4,5},{5,4},{6,7},{7,6},{8,9},{9,8},{10,11... | collective-permute-start | bytes 983048 | tf_op jit(solution)/shard_map/ppermute | solution.py:22
  45.7 6.6 %collective-permute-start.8 = (bf16[4,80,256]{2,1,0:T(8,128)(2,1)S(1)}, bf16[4,80,256]{2,1,0:T(8,128)(2,1)S(1)}, u32[]{:S(2)}, u32[]{:S(2)}) collective-permute-start(bf16[4,80,256]{2,1,0:T(8,128)(2,1)S(1)} %collective-permute-done.2.refs_3_), channel_id=1, source_target_pairs={{0,8},{8,128},{128,136},{136,0},{1,9},{9,129},{129,137},{137,1},{2... | collective-permute-start | bytes 491528 | tf_op jit(solution)/shard_map/ppermute | solution.py:22
  46.5 7.0 %collective-permute-start.9 = (bf16[4,80,256]{2,1,0:T(8,128)(2,1)S(1)}, bf16[4,80,256]{2,1,0:T(8,128)(2,1)S(1)}, u32[]{:S(2)}, u32[]{:S(2)}) collective-permute-start(bf16[4,80,256]{2,1,0:T(8,128)(2,1)S(1)} %collective-permute-done.3.refs_4_), channel_id=1, source_target_pairs={{0,136},{8,0},{128,8},{136,128},{1,137},{9,1},{129,9},{137,129},{2... | collective-permute-start | bytes 491528 | tf_op jit(solution)/shard_map/ppermute | solution.py:22
  48.4 5.8 %collective-permute-start.13 = (bf16[4,80,256]{2,1,0:T(8,128)(2,1)S(1)}, bf16[4,80,256]{2,1,0:T(8,128)(2,1)S(1)}, u32[]{:S(2)}, u32[]{:S(2)}) collective-permute-start(bf16[4,80,256]{2,1,0:T(8,128)(2,1)S(1)} %collective-permute-done.2.refs_3_), channel_id=1, source_target_pairs={{0,1},{1,0},{2,3},{3,2},{4,5},{5,4},{6,7},{7,6},{8,9},{9,8},{10,11... | collective-permute-start | bytes 491528 | tf_op jit(solution)/shard_map/ppermute | solution.py:22
  58.7 5.7 %collective-permute-start.21 = (bf16[80,1024]{1,0:T(8,128)(2,1)S(1)}, bf16[80,1024]{1,0:T(8,128)(2,1)S(1)}, u32[]{:S(2)}, u32[]{:S(2)}) collective-permute-start(bf16[80,1024]{1,0:T(8,128)(2,1)S(1)} %shard_map.30.unit.refs_0_), channel_id=1, source_target_pairs={{128,112},{144,96},{160,80},{176,64},{64,176},{80,160},{96,144},{1... | collective-permute-start | bytes 491528 | tf_op jit(solution)/shard_map/ppermute | solution.py:206
  59.4 12.1 %collective-permute-start.26 = (bf16[80,1024]{1,0:T(8,128)(2,1)S(1)}, bf16[80,1024]{1,0:T(8,128)(2,1)S(1)}, u32[]{:S(2)}, u32[]{:S(2)}) collective-permute-start(bf16[80,1024]{1,0:T(8,128)(2,1)S(1)} %shard_map.30.unit.refs_0_), channel_id=1, source_target_pairs={{0,128},{8,136},{128,0},{136,8},{1,129},{9,137},{129,1},{137,9},{2... | collective-permute-start | bytes 491528 | tf_op jit(solution)/shard_map/ppermute | solution.py:22
  62.9 11.6 %collective-permute-start.25 = (bf16[80,1024]{1,0:T(8,128)(2,1)S(1)}, bf16[80,1024]{1,0:T(8,128)(2,1)S(1)}, u32[]{:S(2)}, u32[]{:S(2)}) collective-permute-start(bf16[80,1024]{1,0:T(8,128)(2,1)S(1)} %shard_map.30.unit.refs_0_), channel_id=1, source_target_pairs={{0,136},{8,0},{128,8},{136,128},{1,137},{9,1},{129,9},{137,129},{2... | collective-permute-start | bytes 491528 | tf_op jit(solution)/shard_map/ppermute | solution.py:22
  63.0 11.5 %collective-permute-start.24 = (bf16[80,1024]{1,0:T(8,128)(2,1)S(1)}, bf16[80,1024]{1,0:T(8,128)(2,1)S(1)}, u32[]{:S(2)}, u32[]{:S(2)}) collective-permute-start(bf16[80,1024]{1,0:T(8,128)(2,1)S(1)} %shard_map.30.unit.refs_0_), channel_id=1, source_target_pairs={{0,8},{8,128},{128,136},{136,0},{1,9},{9,129},{129,137},{137,1},{2... | collective-permute-start | bytes 491528 | tf_op jit(solution)/shard_map/ppermute | solution.py:22
  65.0 9.6 %collective-permute-start.23 = (bf16[80,1024]{1,0:T(8,128)(2,1)S(1)}, bf16[80,1024]{1,0:T(8,128)(2,1)S(1)}, u32[]{:S(2)}, u32[]{:S(2)}) collective-permute-start(bf16[80,1024]{1,0:T(8,128)(2,1)S(1)} %shard_map.31.refs_0_), channel_id=1, source_target_pairs={{0,112},{16,0},{32,16},{48,32},{64,48},{80,64},{96,80},{112,96},{1... | collective-permute-start | bytes 491528 | tf_op jit(solution)/shard_map/ppermute | solution.py:22
  71.4 5.4 %collective-permute-start.22 = (bf16[80,1024]{1,0:T(8,128)(2,1)S(1)}, bf16[80,1024]{1,0:T(8,128)(2,1)S(1)}, u32[]{:S(2)}, u32[]{:S(2)}) collective-permute-start(bf16[80,1024]{1,0:T(8,128)(2,1)S(1)} %shard_map.31.refs_0_), channel_id=1, source_target_pairs={{0,16},{16,32},{32,48},{48,64},{64,80},{80,96},{96,112},{112,0},{1... | collective-permute-start | bytes 491528 | tf_op jit(solution)/shard_map/ppermute | solution.py:22
  76.9 15.6 %collective-permute-start.32 = (bf16[4,80,1024]{2,1,0:T(8,128)(2,1)S(1)}, bf16[4,80,1024]{2,1,0:T(8,128)(2,1)S(1)}, u32[]{:S(2)}, u32[]{:S(2)}) collective-permute-start(bf16[4,80,1024]{2,1,0:T(8,128)(2,1)S(1)} %shard_map.32.near), channel_id=1, source_target_pairs={{0,6},{2,0},{4,2},{6,4},{1,7},{3,1},{5,3},{7,5},{8,14},{10,8},{12,... | collective-permute-start | bytes 1966088 | tf_op jit(solution)/shard_map/ppermute | solution.py:22
  79.8 12.8 %collective-permute-start.31 = (bf16[4,80,1024]{2,1,0:T(8,128)(2,1)S(1)}, bf16[4,80,1024]{2,1,0:T(8,128)(2,1)S(1)}, u32[]{:S(2)}, u32[]{:S(2)}) collective-permute-start(bf16[4,80,1024]{2,1,0:T(8,128)(2,1)S(1)} %shard_map.32.near), channel_id=1, source_target_pairs={{0,2},{2,4},{4,6},{6,0},{1,3},{3,5},{5,7},{7,1},{8,10},{10,12},{12... | collective-permute-start | bytes 1966088 | tf_op jit(solution)/shard_map/ppermute | solution.py:22
  79.8 5.4 %collective-permute-start.27 = (bf16[80,1024]{1,0:T(8,128)(2,1)S(1)}, bf16[80,1024]{1,0:T(8,128)(2,1)S(1)}, u32[]{:S(2)}, u32[]{:S(2)}) collective-permute-start(bf16[80,1024]{1,0:T(8,128)(2,1)S(1)} %collective-permute-done.22.refs_1_), channel_id=1, source_target_pairs={{0,16},{16,32},{32,48},{48,64},{64,80},{80,96},{96,112},{112,0},{1... | collective-permute-start | bytes 491528 | tf_op jit(solution)/shard_map/ppermute | solution.py:22
  85.2 7.4 %collective-permute-start.28 = (bf16[80,1024]{1,0:T(8,128)(2,1)S(1)}, bf16[80,1024]{1,0:T(8,128)(2,1)S(1)}, u32[]{:S(2)}, u32[]{:S(2)}) collective-permute-start(bf16[80,1024]{1,0:T(8,128)(2,1)S(1)} %collective-permute-done.27.refs_3_), channel_id=1, source_target_pairs={{0,16},{16,32},{32,48},{48,64},{64,80},{80,96},{96,112},{112,0},{1... | collective-permute-start | bytes 491528 | tf_op jit(solution)/shard_map/ppermute | solution.py:22
  85.2 7.4 %collective-permute-start.30 = (bf16[80,1024]{1,0:T(8,128)(2,1)S(1)}, bf16[80,1024]{1,0:T(8,128)(2,1)S(1)}, u32[]{:S(2)}, u32[]{:S(2)}) collective-permute-start(bf16[80,1024]{1,0:T(8,128)(2,1)S(1)} %collective-permute-done.29.refs_4_), channel_id=1, source_target_pairs={{0,112},{16,0},{32,16},{48,32},{64,48},{80,64},{96,80},{112,96},{1... | collective-permute-start | bytes 491528 | tf_op jit(solution)/shard_map/ppermute | solution.py:22
  92.6 17.6 %collective-permute-start.34 = (bf16[2,80,1024]{2,1,0:T(8,128)(2,1)S(1)}, bf16[2,80,1024]{2,1,0:T(8,128)(2,1)S(1)}, u32[]{:S(2)}, u32[]{:S(2)}) collective-permute-start(bf16[2,80,1024]{2,1,0:T(8,128)(2,1)S(1)} %get-tuple-element.51), channel_id=1, source_target_pairs={{0,2},{2,4},{4,6},{6,0},{1,3},{3,5},{5,7},{7,1},{8,10},{10,12},{12... | collective-permute-start | bytes 983048 | tf_op jit(solution)/shard_map/ppermute | solution.py:22
  92.9 17.2 %collective-permute-start.35 = (bf16[2,80,1024]{2,1,0:T(8,128)(2,1)S(1)}, bf16[2,80,1024]{2,1,0:T(8,128)(2,1)S(1)}, u32[]{:S(2)}, u32[]{:S(2)}) collective-permute-start(bf16[2,80,1024]{2,1,0:T(8,128)(2,1)S(1)} %get-tuple-element.52), channel_id=1, source_target_pairs={{0,6},{2,0},{4,2},{6,4},{1,7},{3,1},{5,3},{7,5},{8,14},{10,8},{12,... | collective-permute-start | bytes 983048 | tf_op jit(solution)/shard_map/ppermute | solution.py:22
  95.6 8.1 %collective-permute-start.33 = (bf16[80,1024]{1,0:T(8,128)(2,1)S(1)}, bf16[80,1024]{1,0:T(8,128)(2,1)S(1)}, u32[]{:S(2)}, u32[]{:S(2)}) collective-permute-start(bf16[80,1024]{1,0:T(8,128)(2,1)S(1)} %collective-permute-done.28.refs_5_), channel_id=1, source_target_pairs={{0,16},{16,32},{32,48},{48,64},{64,80},{80,96},{96,112},{112,0},{1... | collective-permute-start | bytes 491528 | tf_op jit(solution)/shard_map/ppermute | solution.py:22
  96.9 13.8 %collective-permute-start.36 = (bf16[80,1024]{1,0:T(8,128)(2,1)S(1)}, bf16[80,1024]{1,0:T(8,128)(2,1)S(1)}, u32[]{:S(2)}, u32[]{:S(2)}) collective-permute-start(bf16[80,1024]{1,0:T(8,128)(2,1)S(1)} %shard_map.31.refs_0_), channel_id=1, source_target_pairs={{0,1},{1,0},{2,3},{3,2},{4,5},{5,4},{6,7},{7,6},{8,9},{9,8},{10,11... | collective-permute-start | bytes 491528 | tf_op jit(solution)/shard_map/ppermute | solution.py:22
  103.6 7.1 %collective-permute-start.37 = (bf16[80,1024]{1,0:T(8,128)(2,1)S(1)}, bf16[80,1024]{1,0:T(8,128)(2,1)S(1)}, u32[]{:S(2)}, u32[]{:S(2)}) collective-permute-start(bf16[80,1024]{1,0:T(8,128)(2,1)S(1)} %collective-permute-done.22.refs_1_), channel_id=1, source_target_pairs={{0,1},{1,0},{2,3},{3,2},{4,5},{5,4},{6,7},{7,6},{8,9},{9,8},{10,11... | collective-permute-start | bytes 491528 | tf_op jit(solution)/shard_map/ppermute | solution.py:22
  103.6 7.6 %collective-permute-start.38 = (bf16[80,1024]{1,0:T(8,128)(2,1)S(1)}, bf16[80,1024]{1,0:T(8,128)(2,1)S(1)}, u32[]{:S(2)}, u32[]{:S(2)}) collective-permute-start(bf16[80,1024]{1,0:T(8,128)(2,1)S(1)} %collective-permute-done.23.refs_2_), channel_id=1, source_target_pairs={{0,1},{1,0},{2,3},{3,2},{4,5},{5,4},{6,7},{7,6},{8,9},{9,8},{10,11... | collective-permute-start | bytes 491528 | tf_op jit(solution)/shard_map/ppermute | solution.py:22
  (14 other events, 58.1 us)

commit v2 on v1

--- a/solution.py
+++ b/solution.py
@@ -10,7 +10,6 @@
 Y = ("yh", "yl")
 ROWS, OCC, AUX, BASIS = 80, 256, 4, 10240
 DEPTH = AUX * OCC
-RING4 = (0, 3, 1, 2)
 RING8 = (0, 7, 1, 6, 2, 5, 3, 4)
 MIB = 1 << 20
 VMEM = pl.BlockSpec(memory_space=pltpu.VMEM)
@@ -101,18 +100,6 @@
     )[0]
 
 
-def held_kernel(where, unit, moved, out):
-    home = where[0] == where[2] // 4
-
-    @pl.when(home)
-    def _():
-        out[...] = unit[...]
-
-    @pl.when(jnp.logical_not(home))
-    def _():
-        out[...] = moved[...]
-
-
 def stack_kernel(*refs):
     for i, ref in enumerate(refs[:-1]):
         refs[-1][i] = ref[...]
@@ -124,37 +111,34 @@
 
 def product_kernel(where, near, left, right, far0, far1, *refs):
     cols, (out, lefts, rights) = refs[:16], refs[16:]
-    yh, yl, z, x, c = (where[i] for i in range(5))
-    for ref, along_x, first in ((near, 0, 0), (left, 3, 0), (right, 1, 0), (far0, 2, 0), (far1, 2, 2)):
-        at_x = lax.rem(x + along_x, 4)
+    yl, z, x, c = (where[i] for i in range(1, 5))
+    for ref, along_x, first in ((near, 0, 0), (left, 3, 0), (right, 1, 0), (far0, 2, 0), (far1, 2, 1)):
         for i in range(ref.shape[0]):
-            at_y = lax.rem(yh * 2 + yl + RING4[first + i], 4)
-            lefts[at_y // 2, (at_y % 2) * 4 + at_x] = ref[i]
+            side = 1 - yl if first + i else yl
+            lefts[side * 4 + lax.rem(x + along_x, 4)] = ref[i]
     for other in range(2):
         core = 1 - c if other else c
         for ref, along in zip(cols[other * 8:other * 8 + 8], RING8):
-            at_z = lax.rem(z + along, 8)
-            side = at_z // 4
-            q = jnp.where(side == yh, at_z % 4, 3 - at_z % 4)
-            rights[side, q * 2 + core] = ref[...]
-    total = None
-    for side in range(2):
-        part = lax.dot_general(
-            lefts[side].reshape(640, DEPTH), rights[side].reshape(640, DEPTH),
-            (((1,), (1,)), ((), ())), preferred_element_type=jnp.float32,
-        )
-        total = part if total is None else total + part
-    out[...] = total.astype(jnp.bfloat16).reshape(8, ROWS, 640)
+            rights[lax.rem(z + along, 8), core] = ref[...]
+    block = lax.dot_general(
+        lefts[...].reshape(640, DEPTH), rights[...].reshape(1280, DEPTH),
+        (((1,), (1,)), ((), ())), preferred_element_type=jnp.float32,
+    ).astype(jnp.bfloat16)
+    for h in range(2):
+        out[h * 8:(h + 1) * 8] = block[:, h * 640:(h + 1) * 640].reshape(8, ROWS, 640)
 
 
 def product(where, rows, cols):
     return call(
         product_kernel,
-        [(8, ROWS, 640)],
+        [(16, ROWS, 640)],
         [(SMEM, where)] + [(VMEM, v) for v in rows + cols],
-        16,
-        [pltpu.VMEM((2, 8, ROWS, DEPTH), jnp.bfloat16)] * 2,
-        2 * 640 * 640 * 2 * DEPTH, 6 * MIB,
+        20,
+        [
+            pltpu.VMEM((8, ROWS, DEPTH), jnp.bfloat16),
+            pltpu.VMEM((8, 2, ROWS, DEPTH), jnp.bfloat16),
+        ],
+        2 * 640 * 1280 * DEPTH, 6 * MIB,
     )[0]
 
 
@@ -162,7 +146,8 @@
     for q in range(4):
         for s in range(8):
             at = q * 1280 + s * 160
-            out[:, at:at + 160] = pieces[s, :, q * 160:(q + 1) * 160].astype(jnp.float32)
+            lanes = slice(q * 160, (q + 1) * 160)
+            out[:, at:at + 160] = pieces[s, :, lanes].astype(jnp.float32) + pieces[8 + s, :, lanes].astype(jnp.float32)
 
 
 def spread(pieces):
@@ -199,17 +184,10 @@
     pieces += [swap(p) for p in pieces]
     unit = transform(where, flat, pieces)
 
-    moves = []
-    for zi in range(8):
-        home = zi // 4
-        moves.append(((1 - home) * 8 + zi, home * 8 + 7 - zi))
-    moved = lax.ppermute(unit, ("yh", "z"), moves)
-    at_y = stack(unit, shift(unit, Y, 1), shift(unit, Y, -1), shift(unit, Y, 2))
-    held = call(held_kernel, [unit.shape], [(SMEM, where), (VMEM, unit), (VMEM, moved)], 4)[0]
-
-    up, down = shift(held, "z", 1), shift(held, "z", -1)
-    up, down, at_y = together(up, down, at_y)
-    left, right = shift(at_y, "x", 1), shift(at_y, "x", -1)
+    ynear = shift(unit, "yl", 1)
+    up, down = shift(unit, "z", 1), shift(unit, "z", -1)
+    near = stack(unit, ynear)
+    left, right = shift(near, "x", 1), shift(near, "x", -1)
     up2, down2 = shift(up, "z", 1), shift(down, "z", -1)
     up3, down3 = shift(up2, "z", 1), shift(down2, "z", -1)
     up3, down3, left, right = together(up3, down3, left, right)
@@ -217,11 +195,11 @@
     far = [shift(far[0], "x", 1), shift(far[1], "x", -1)]
     up4 = shift(up3, "z", 1)
     up4, *far = together(up4, *far)
-    cols = [held, up, down, up2, down2, up3, down3, up4]
+    cols = [unit, up, down, up2, down2, up3, down3, up4]
     cols += [swap(v) for v in cols]
 
-    block = product(where, [at_y, left, right, *far], cols)
-    return spread(lax.all_to_all(block, ("yl", "x"), split_axis=0, concat_axis=0, tiled=True))
+    block = product(where, [near, left, right, *far], cols)
+    return spread(lax.all_to_all(block, ("yh", "yl", "x"), split_axis=0, concat_axis=0, tiled=True))
 
 
 def solution(mesh):

time: 134 us -> 124 us (0.925)
  starting transfers between devices: 64 us -> 43.6 us
  blocking collectives: 36.5 us -> 49.2 us
    ppermute x43 -> x41, starting transfers between devices: 63.4 us -> 43.6 us  [shift(): lax.ppermute(value, axis, [(i, (i + by) % count) for i in range(count)])]
    all_to_all x1, blocking collectives: 16 us -> 28.7 us  [per_device(): lax.all_to_all(block, ('yh', 'yl', 'x'), split_axis=0, concat_axis=0, til...]
    pallas_call x7 -> x6, Pallas kernels: 6.61 us -> 5.49 us  [call(): pl.pallas_call(kernel, out_shape=shapes, in_specs=[spec for spec, _ in in...]
    ppermute x43 -> x41, waiting for transfers between devices: 20.7 us -> 20 us  [shift(): lax.ppermute(value, axis, [(i, (i + by) % count) for i in range(count)])]
  transfers between devices with their start and end apart: 44 -> 41, of which waited for: 13 -> 14; matrix products, arithmetic and copies ran while one was open for 0% -> 0% of each run, Pallas kernels for 0% -> 0%
where the time goes in v2:
time: 124 us
  blocking collectives  49.2 us (40%)
  starting transfers between devices  43.6 us (35%)
  waiting for transfers between devices  20 us (16%)
  Pallas kernels  7.23 us (6%)
  local copies, waits for them, and re-layouts  3.75 us (3%)
    ppermute x41, starting transfers between devices, shift(): lax.ppermute(value, axis, [(i, (i + by) % count) for i in range(count)])  43.6 us
    all_to_all x1, blocking collectives, per_device(): lax.all_to_all(block, ('yh', 'yl', 'x'), split_axis=0, concat_axis=0, til...  28.7 us
    all_to_all x1, blocking collectives, everywhere(): return lax.all_to_all(copies, axes, split_axis=0, concat_axis=0, tiled=True)  20.5 us
    ppermute x41, waiting for transfers between devices, shift(): lax.ppermute(value, axis, [(i, (i + by) % count) for i in range(count)])  20 us
    pallas_call x6, Pallas kernels, call(): pl.pallas_call(kernel, out_shape=shapes, in_specs=[spec for spec, _ in in...  5.49 us
    unnamed x4, local copies, waits for them, and re-layouts  2.86 us
  transfers between devices with their start and end apart: 41, of which 14 were waited for; matrix products, arithmetic and copies ran while one was open for 0% of the time, Pallas kernels for 0%

profile of v2, /device:TPU:1, one launch (start us, length us, event | category | flops | bytes accessed | tf_op | source)
XLA Modules:
  0.0 123.9 jit_solution(1557108705909355083)
XLA Ops:
  0.1 0.8 broadcast_in_dim.2
  0.9 20.5 %all_to_all.10.first.second.refs_0_ = bf16[8,80,256]{2,1,0:T(8,128)(2,1)S(1)} all-to-all(bf16[8,80,256]{2,1,0:T(8,128)(2,1)S(1)} %broadcast_in_dim.2), channel_id=1, replica_groups=mesh['yh'=2,'z'=8,'yl'=2,'x'=4,'c'=2] {'z'}, dimensions={0} | all-to-all | bytes 655360 | tf_op jit(solution)/shard_map/all_to_all | solution.py:48
  21.4 2.5 %collective-permute-start.1 = (bf16[8,80,256]{2,1,0:T(8,128)(2,1)S(1)}, bf16[8,80,256]{2,1,0:T(8,128)(2,1)S(1)}, u32[]{:S(2)}, u32[]{:S(2)}) collective-permute-start(bf16[8,80,256]{2,1,0:T(8,128)(2,1)S(1)} %all_to_all.10.first.second.refs_0_), channel_id=1, source_target_pairs={{0,6},{2,0},{4,2},{6,4},{1,7},{3,1},{5,3},{7,5},{8,14},{10,8},{12,... | collective-permute-start | bytes 983048 | tf_op jit(solution)/shard_map/ppermute | solution.py:21
  23.9 2.9 %copy-done = bf16[4,80,10240]{2,1,0:T(8,128)(2,1)S(1)} copy-done((bf16[4,80,10240]{2,1,0:T(8,128)(2,1)S(1)}, bf16[4,80,10240]{2,1,0:T(8,128)(2,1)}, u32[]{:S(2)}) %copy-start) | copy-done | bytes 6553624
  26.7 1.4 %collective-permute-start.6 = (bf16[4,80,256]{2,1,0:T(8,128)(2,1)S(1)}, bf16[4,80,256]{2,1,0:T(8,128)(2,1)S(1)}, u32[]{:S(2)}, u32[]{:S(2)}) collective-permute-start(bf16[4,80,256]{2,1,0:T(8,128)(2,1)S(1)} %get-tuple-element.36), channel_id=1, source_target_pairs={{0,8},{8,128},{128,136},{136,0},{1,9},{9,129},{129,137},{137,1},{2... | collective-permute-start | bytes 491528 | tf_op jit(solution)/shard_map/ppermute | solution.py:21
  28.1 1.5 %collective-permute-start.7 = (bf16[4,80,256]{2,1,0:T(8,128)(2,1)S(1)}, bf16[4,80,256]{2,1,0:T(8,128)(2,1)S(1)}, u32[]{:S(2)}, u32[]{:S(2)}) collective-permute-start(bf16[4,80,256]{2,1,0:T(8,128)(2,1)S(1)} %get-tuple-element.37), channel_id=1, source_target_pairs={{0,136},{8,0},{128,8},{136,128},{1,137},{9,1},{129,9},{137,129},{2... | collective-permute-start | bytes 491528 | tf_op jit(solution)/shard_map/ppermute | solution.py:21
  29.6 1.8 %collective-permute-done.first.refs_1_ = bf16[8,80,256]{2,1,0:T(8,128)(2,1)S(1)} collective-permute-done((bf16[8,80,256]{2,1,0:T(8,128)(2,1)S(1)}, bf16[8,80,256]{2,1,0:T(8,128)(2,1)S(1)}, u32[]{:S(2)}, u32[]{:S(2)}) %collective-permute-start) | collective-permute-done | bytes 327712 | tf_op jit(solution)/shard_map/ppermute | solution.py:21
  31.4 1.3 %collective-permute-start.4 = (bf16[8,80,256]{2,1,0:T(8,128)(2,1)S(1)}, bf16[8,80,256]{2,1,0:T(8,128)(2,1)S(1)}, u32[]{:S(2)}, u32[]{:S(2)}) collective-permute-start(bf16[8,80,256]{2,1,0:T(8,128)(2,1)S(1)} %collective-permute-done.first.refs_1_), channel_id=1, source_target_pairs={{0,8},{8,128},{128,136},{136,0},{1,9},{9,129},{129,137},{137,1},{2... | collective-permute-start | bytes 983048 | tf_op jit(solution)/shard_map/ppermute | solution.py:21
  32.7 1.4 %collective-permute-start.5 = (bf16[8,80,256]{2,1,0:T(8,128)(2,1)S(1)}, bf16[8,80,256]{2,1,0:T(8,128)(2,1)S(1)}, u32[]{:S(2)}, u32[]{:S(2)}) collective-permute-start(bf16[8,80,256]{2,1,0:T(8,128)(2,1)S(1)} %collective-permute-done.1.second.refs_2_), channel_id=1, source_target_pairs={{0,136},{8,0},{128,8},{136,128},{1,137},{9,1},{129,9},{137,129},{2... | collective-permute-start | bytes 983048 | tf_op jit(solution)/shard_map/ppermute | solution.py:21
  34.3 2.7 %collective-permute-start.3 = (bf16[4,80,256]{2,1,0:T(8,128)(2,1)S(1)}, bf16[4,80,256]{2,1,0:T(8,128)(2,1)S(1)}, u32[]{:S(2)}, u32[]{:S(2)}) collective-permute-start(bf16[4,80,256]{2,1,0:T(8,128)(2,1)S(1)} %get-tuple-element.33), channel_id=1, source_target_pairs={{0,6},{2,0},{4,2},{6,4},{1,7},{3,1},{5,3},{7,5},{8,14},{10,8},{12,... | collective-permute-start | bytes 491528 | tf_op jit(solution)/shard_map/ppermute | solution.py:21
  36.9 4.8 %collective-permute-start.10 = (bf16[8,80,256]{2,1,0:T(8,128)(2,1)S(1)}, bf16[8,80,256]{2,1,0:T(8,128)(2,1)S(1)}, u32[]{:S(2)}, u32[]{:S(2)}) collective-permute-start(bf16[8,80,256]{2,1,0:T(8,128)(2,1)S(1)} %all_to_all.10.first.second.refs_0_), channel_id=1, source_target_pairs={{0,1},{1,0},{2,3},{3,2},{4,5},{5,4},{6,7},{7,6},{8,9},{9,8},{10,11... | collective-permute-start | bytes 983048 | tf_op jit(solution)/shard_map/ppermute | solution.py:21
  41.8 3.3 %collective-permute-start.15 = (bf16[4,80,256]{2,1,0:T(8,128)(2,1)S(1)}, bf16[4,80,256]{2,1,0:T(8,128)(2,1)S(1)}, u32[]{:S(2)}, u32[]{:S(2)}) collective-permute-start(bf16[4,80,256]{2,1,0:T(8,128)(2,1)S(1)} %collective-permute-done.6.refs_5_), channel_id=1, source_target_pairs={{0,1},{1,0},{2,3},{3,2},{4,5},{5,4},{6,7},{7,6},{8,9},{9,8},{10,11... | collective-permute-start | bytes 491528 | tf_op jit(solution)/shard_map/ppermute | solution.py:21
  46.5 2.3 %collective-permute-start.9 = (bf16[4,80,256]{2,1,0:T(8,128)(2,1)S(1)}, bf16[4,80,256]{2,1,0:T(8,128)(2,1)S(1)}, u32[]{:S(2)}, u32[]{:S(2)}) collective-permute-start(bf16[4,80,256]{2,1,0:T(8,128)(2,1)S(1)} %collective-permute-done.3.refs_4_), channel_id=1, source_target_pairs={{0,136},{8,0},{128,8},{136,128},{1,137},{9,1},{129,9},{137,129},{2... | collective-permute-start | bytes 491528 | tf_op jit(solution)/shard_map/ppermute | solution.py:21
  48.8 0.9 collective-permute-start.13
  49.7 3.0 %collective-permute-done.8.refs_9_ = bf16[4,80,256]{2,1,0:T(8,128)(2,1)S(1)} collective-permute-done((bf16[4,80,256]{2,1,0:T(8,128)(2,1)S(1)}, bf16[4,80,256]{2,1,0:T(8,128)(2,1)S(1)}, u32[]{:S(2)}, u32[]{:S(2)}) %collective-permute-start.8) | collective-permute-done | bytes 163872 | tf_op jit(solution)/shard_map/ppermute | solution.py:21
  52.7 1.2 collective-permute-start.17
  55.0 0.9 collective-permute-done.14.refs_15_
  56.4 2.8 %shard_map.30.refs_0_ = bf16[80,1024]{1,0:T(8,128)(2,1)S(1)} custom-call(s32[5]{0:T(128)S(1)} %stack.23.where, bf16[320,10240]{1,0:T(8,128)(2,1)S(1)} %bitcast.7, bf16[8,80,256]{2,1,0:T(8,128)(2,1)S(1)} %all_to_all.10.first.second.refs_0_, bf16[8,80,256]{2,1,0:T(8,128)(2,1)S(1)} %collective-permute-done.first.refs_1_, ...), custom_call_target="tpu_custom_call" | custom-call | flops 1677721600 | bytes 12582912 | tf_op jit(solution)/shard_map/pallas_call | solution.py:34
  59.3 1.5 %collective-permute-start.22 = (bf16[80,1024]{1,0:T(8,128)(2,1)S(1)}, bf16[80,1024]{1,0:T(8,128)(2,1)S(1)}, u32[]{:S(2)}, u32[]{:S(2)}) collective-permute-start(bf16[80,1024]{1,0:T(8,128)(2,1)S(1)} %shard_map.30.refs_0_), channel_id=1, source_target_pairs={{0,16},{16,32},{32,48},{48,64},{64,80},{80,96},{96,112},{112,0},{1... | collective-permute-start | bytes 491528 | tf_op jit(solution)/shard_map/ppermute | solution.py:21
  60.8 3.9 %collective-permute-done.21.refs_1_ = bf16[80,1024]{1,0:T(8,128)(2,1)S(1)} collective-permute-done((bf16[80,1024]{1,0:T(8,128)(2,1)S(1)}, bf16[80,1024]{1,0:T(8,128)(2,1)S(1)}, u32[]{:S(2)}, u32[]{:S(2)}) %collective-permute-start.21) | collective-permute-done | bytes 163872 | tf_op jit(solution)/shard_map/ppermute | solution.py:21
  64.6 2.5 %collective-permute-start.29 = (bf16[2,80,1024]{2,1,0:T(8,128)(2,1)S(1)}, bf16[2,80,1024]{2,1,0:T(8,128)(2,1)S(1)}, u32[]{:S(2)}, u32[]{:S(2)}) collective-permute-start(bf16[2,80,1024]{2,1,0:T(8,128)(2,1)S(1)} %shard_map.31.near), channel_id=1, source_target_pairs={{0,6},{2,0},{4,2},{6,4},{1,7},{3,1},{5,3},{7,5},{8,14},{10,8},{12,... | collective-permute-start | bytes 983048 | tf_op jit(solution)/shard_map/ppermute | solution.py:21
  67.2 1.5 %collective-permute-start.23 = (bf16[80,1024]{1,0:T(8,128)(2,1)S(1)}, bf16[80,1024]{1,0:T(8,128)(2,1)S(1)}, u32[]{:S(2)}, u32[]{:S(2)}) collective-permute-start(bf16[80,1024]{1,0:T(8,128)(2,1)S(1)} %collective-permute-done.22.refs_1_), channel_id=1, source_target_pairs={{0,16},{16,32},{32,48},{48,64},{64,80},{80,96},{96,112},{112,0},{1... | collective-permute-start | bytes 491528 | tf_op jit(solution)/shard_map/ppermute | solution.py:21
  68.7 3.0 %collective-permute-done.26.refs_4_ = bf16[80,1024]{1,0:T(8,128)(2,1)S(1)} collective-permute-done((bf16[80,1024]{1,0:T(8,128)(2,1)S(1)}, bf16[80,1024]{1,0:T(8,128)(2,1)S(1)}, u32[]{:S(2)}, u32[]{:S(2)}) %collective-permute-start.26) | collective-permute-done | bytes 163872 | tf_op jit(solution)/shard_map/ppermute | solution.py:21
  71.7 1.2 %collective-permute-start.27 = (bf16[80,1024]{1,0:T(8,128)(2,1)S(1)}, bf16[80,1024]{1,0:T(8,128)(2,1)S(1)}, u32[]{:S(2)}, u32[]{:S(2)}) collective-permute-start(bf16[80,1024]{1,0:T(8,128)(2,1)S(1)} %collective-permute-done.26.refs_4_), channel_id=1, source_target_pairs={{0,112},{16,0},{32,16},{48,32},{64,48},{80,64},{96,80},{112,96},{1... | collective-permute-start | bytes 491528 | tf_op jit(solution)/shard_map/ppermute | solution.py:21
  73.1 3.0 %collective-permute-done.28.first.left = bf16[2,80,1024]{2,1,0:T(8,128)(2,1)S(1)} collective-permute-done((bf16[2,80,1024]{2,1,0:T(8,128)(2,1)S(1)}, bf16[2,80,1024]{2,1,0:T(8,128)(2,1)S(1)}, u32[]{:S(2)}, u32[]{:S(2)}) %collective-permute-start.28) | collective-permute-done | bytes 327712 | tf_op jit(solution)/shard_map/ppermute | solution.py:21
  76.1 2.2 %collective-permute-done.24.refs_5_ = bf16[80,1024]{1,0:T(8,128)(2,1)S(1)} collective-permute-done((bf16[80,1024]{1,0:T(8,128)(2,1)S(1)}, bf16[80,1024]{1,0:T(8,128)(2,1)S(1)}, u32[]{:S(2)}, u32[]{:S(2)}) %collective-permute-start.24) | collective-permute-done | bytes 163872 | tf_op jit(solution)/shard_map/ppermute | solution.py:21
  78.4 3.0 %collective-permute-start.32 = (bf16[1,80,1024]{2,1,0:T(8,128)(2,1)S(1)}, bf16[1,80,1024]{2,1,0:T(8,128)(2,1)S(1)}, u32[]{:S(2)}, u32[]{:S(2)}) collective-permute-start(bf16[1,80,1024]{2,1,0:T(8,128)(2,1)S(1)} %get-tuple-element.46), channel_id=1, source_target_pairs={{0,6},{2,0},{4,2},{6,4},{1,7},{3,1},{5,3},{7,5},{8,14},{10,8},{12,... | collective-permute-start | bytes 491528 | tf_op jit(solution)/shard_map/ppermute | solution.py:21
  81.4 4.0 %collective-permute-start.33 = (bf16[80,1024]{1,0:T(8,128)(2,1)S(1)}, bf16[80,1024]{1,0:T(8,128)(2,1)S(1)}, u32[]{:S(2)}, u32[]{:S(2)}) collective-permute-start(bf16[80,1024]{1,0:T(8,128)(2,1)S(1)} %shard_map.30.refs_0_), channel_id=1, source_target_pairs={{0,1},{1,0},{2,3},{3,2},{4,5},{5,4},{6,7},{7,6},{8,9},{9,8},{10,11... | collective-permute-start | bytes 491528 | tf_op jit(solution)/shard_map/ppermute | solution.py:21
  85.5 2.9 %collective-permute-start.34 = (bf16[80,1024]{1,0:T(8,128)(2,1)S(1)}, bf16[80,1024]{1,0:T(8,128)(2,1)S(1)}, u32[]{:S(2)}, u32[]{:S(2)}) collective-permute-start(bf16[80,1024]{1,0:T(8,128)(2,1)S(1)} %collective-permute-done.22.refs_1_), channel_id=1, source_target_pairs={{0,1},{1,0},{2,3},{3,2},{4,5},{5,4},{6,7},{7,6},{8,9},{9,8},{10,11... | collective-permute-start | bytes 491528 | tf_op jit(solution)/shard_map/ppermute | solution.py:21
  90.8 2.6 %shard_map.33 = bf16[16,80,640]{2,1,0:T(8,128)(2,1)S(1)} custom-call(s32[5]{0:T(128)S(1)} %stack.23.where, bf16[2,80,1024]{2,1,0:T(8,128)(2,1)S(1)} %shard_map.31.near, bf16[2,80,1024]{2,1,0:T(8,128)(2,1)S(1)} %collective-permute-done.28.first.left, bf16[2,80,1024]{2,1,0:T(8,128)(2,1)S(1)} %collective-permute-done.29.second.right, ...), custom_call_target="tpu_custom_call" | custom-call | flops 1677721600 | bytes 6291456 | tf_op jit(solution)/shard_map/pallas_call | solution.py:34
  93.5 28.7 %all_to_all.11.pieces = bf16[16,80,640]{2,1,0:T(8,128)(2,1)S(1)} all-to-all(bf16[16,80,640]{2,1,0:T(8,128)(2,1)S(1)} %shard_map.33), channel_id=1, replica_groups=mesh['yh'=2,'z'=8,'yl'=2,'x'=4,'c'=2] {'yh','yl','x'}, dimensions={0} | all-to-all | bytes 3276800 | tf_op jit(solution)/shard_map/all_to_all | solution.py:202
  122.2 1.7 %shard_map.34 = f32[80,5120]{1,0:T(8,128)} custom-call(bf16[16,80,640]{2,1,0:T(8,128)(2,1)S(1)} %all_to_all.11.pieces), custom_call_target="tpu_custom_call" | custom-call | bytes 4194304 | tf_op jit(solution)/shard_map/pallas_call | solution.py:154
  (65 shorter events, 6.1 us)
Async XLA Ops:
  21.4 8.3 %collective-permute-start.1 = (bf16[8,80,256]{2,1,0:T(8,128)(2,1)S(1)}, bf16[8,80,256]{2,1,0:T(8,128)(2,1)S(1)}, u32[]{:S(2)}, u32[]{:S(2)}) collective-permute-start(bf16[8,80,256]{2,1,0:T(8,128)(2,1)S(1)} %all_to_all.10.first.second.refs_0_), channel_id=1, source_target_pairs={{0,6},{2,0},{4,2},{6,4},{1,7},{3,1},{5,3},{7,5},{8,14},{10,8},{12,... | collective-permute-start | bytes 983048 | tf_op jit(solution)/shard_map/ppermute | solution.py:21
  23.9 7.6 %collective-permute-start = (bf16[8,80,256]{2,1,0:T(8,128)(2,1)S(1)}, bf16[8,80,256]{2,1,0:T(8,128)(2,1)S(1)}, u32[]{:S(2)}, u32[]{:S(2)}) collective-permute-start(bf16[8,80,256]{2,1,0:T(8,128)(2,1)S(1)} %all_to_all.10.first.second.refs_0_), channel_id=1, source_target_pairs={{0,2},{2,4},{4,6},{6,0},{1,3},{3,5},{5,7},{7,1},{8,10},{10,12},{12... | collective-permute-start | bytes 983048 | tf_op jit(solution)/shard_map/ppermute | solution.py:21
  26.7 7.5 %collective-permute-start.6 = (bf16[4,80,256]{2,1,0:T(8,128)(2,1)S(1)}, bf16[4,80,256]{2,1,0:T(8,128)(2,1)S(1)}, u32[]{:S(2)}, u32[]{:S(2)}) collective-permute-start(bf16[4,80,256]{2,1,0:T(8,128)(2,1)S(1)} %get-tuple-element.36), channel_id=1, source_target_pairs={{0,8},{8,128},{128,136},{136,0},{1,9},{9,129},{129,137},{137,1},{2... | collective-permute-start | bytes 491528 | tf_op jit(solution)/shard_map/ppermute | solution.py:21
  28.1 8.8 %collective-permute-start.7 = (bf16[4,80,256]{2,1,0:T(8,128)(2,1)S(1)}, bf16[4,80,256]{2,1,0:T(8,128)(2,1)S(1)}, u32[]{:S(2)}, u32[]{:S(2)}) collective-permute-start(bf16[4,80,256]{2,1,0:T(8,128)(2,1)S(1)} %get-tuple-element.37), channel_id=1, source_target_pairs={{0,136},{8,0},{128,8},{136,128},{1,137},{9,1},{129,9},{137,129},{2... | collective-permute-start | bytes 491528 | tf_op jit(solution)/shard_map/ppermute | solution.py:21
  31.4 13.7 %collective-permute-start.4 = (bf16[8,80,256]{2,1,0:T(8,128)(2,1)S(1)}, bf16[8,80,256]{2,1,0:T(8,128)(2,1)S(1)}, u32[]{:S(2)}, u32[]{:S(2)}) collective-permute-start(bf16[8,80,256]{2,1,0:T(8,128)(2,1)S(1)} %collective-permute-done.first.refs_1_), channel_id=1, source_target_pairs={{0,8},{8,128},{128,136},{136,0},{1,9},{9,129},{129,137},{137,1},{2... | collective-permute-start | bytes 983048 | tf_op jit(solution)/shard_map/ppermute | solution.py:21
  32.7 12.9 %collective-permute-start.5 = (bf16[8,80,256]{2,1,0:T(8,128)(2,1)S(1)}, bf16[8,80,256]{2,1,0:T(8,128)(2,1)S(1)}, u32[]{:S(2)}, u32[]{:S(2)}) collective-permute-start(bf16[8,80,256]{2,1,0:T(8,128)(2,1)S(1)} %collective-permute-done.1.second.refs_2_), channel_id=1, source_target_pairs={{0,136},{8,0},{128,8},{136,128},{1,137},{9,1},{129,9},{137,129},{2... | collective-permute-start | bytes 983048 | tf_op jit(solution)/shard_map/ppermute | solution.py:21
  34.2 7.6 %collective-permute-start.2 = (bf16[4,80,256]{2,1,0:T(8,128)(2,1)S(1)}, bf16[4,80,256]{2,1,0:T(8,128)(2,1)S(1)}, u32[]{:S(2)}, u32[]{:S(2)}) collective-permute-start(bf16[4,80,256]{2,1,0:T(8,128)(2,1)S(1)} %get-tuple-element.32), channel_id=1, source_target_pairs={{0,2},{2,4},{4,6},{6,0},{1,3},{3,5},{5,7},{7,1},{8,10},{10,12},{12... | collective-permute-start | bytes 491528 | tf_op jit(solution)/shard_map/ppermute | solution.py:21
  34.3 10.8 %collective-permute-start.3 = (bf16[4,80,256]{2,1,0:T(8,128)(2,1)S(1)}, bf16[4,80,256]{2,1,0:T(8,128)(2,1)S(1)}, u32[]{:S(2)}, u32[]{:S(2)}) collective-permute-start(bf16[4,80,256]{2,1,0:T(8,128)(2,1)S(1)} %get-tuple-element.33), channel_id=1, source_target_pairs={{0,6},{2,0},{4,2},{6,4},{1,7},{3,1},{5,3},{7,5},{8,14},{10,8},{12,... | collective-permute-start | bytes 491528 | tf_op jit(solution)/shard_map/ppermute | solution.py:21
  36.9 11.8 %collective-permute-start.10 = (bf16[8,80,256]{2,1,0:T(8,128)(2,1)S(1)}, bf16[8,80,256]{2,1,0:T(8,128)(2,1)S(1)}, u32[]{:S(2)}, u32[]{:S(2)}) collective-permute-start(bf16[8,80,256]{2,1,0:T(8,128)(2,1)S(1)} %all_to_all.10.first.second.refs_0_), channel_id=1, source_target_pairs={{0,1},{1,0},{2,3},{3,2},{4,5},{5,4},{6,7},{7,6},{8,9},{9,8},{10,11... | collective-permute-start | bytes 983048 | tf_op jit(solution)/shard_map/ppermute | solution.py:21
  41.8 4.3 %collective-permute-start.15 = (bf16[4,80,256]{2,1,0:T(8,128)(2,1)S(1)}, bf16[4,80,256]{2,1,0:T(8,128)(2,1)S(1)}, u32[]{:S(2)}, u32[]{:S(2)}) collective-permute-start(bf16[4,80,256]{2,1,0:T(8,128)(2,1)S(1)} %collective-permute-done.6.refs_5_), channel_id=1, source_target_pairs={{0,1},{1,0},{2,3},{3,2},{4,5},{5,4},{6,7},{7,6},{8,9},{9,8},{10,11... | collective-permute-start | bytes 491528 | tf_op jit(solution)/shard_map/ppermute | solution.py:21
  45.1 8.9 %collective-permute-start.11 = (bf16[8,80,256]{2,1,0:T(8,128)(2,1)S(1)}, bf16[8,80,256]{2,1,0:T(8,128)(2,1)S(1)}, u32[]{:S(2)}, u32[]{:S(2)}) collective-permute-start(bf16[8,80,256]{2,1,0:T(8,128)(2,1)S(1)} %collective-permute-done.first.refs_1_), channel_id=1, source_target_pairs={{0,1},{1,0},{2,3},{3,2},{4,5},{5,4},{6,7},{7,6},{8,9},{9,8},{10,11... | collective-permute-start | bytes 983048 | tf_op jit(solution)/shard_map/ppermute | solution.py:21
  45.6 8.9 %collective-permute-start.12 = (bf16[8,80,256]{2,1,0:T(8,128)(2,1)S(1)}, bf16[8,80,256]{2,1,0:T(8,128)(2,1)S(1)}, u32[]{:S(2)}, u32[]{:S(2)}) collective-permute-start(bf16[8,80,256]{2,1,0:T(8,128)(2,1)S(1)} %collective-permute-done.1.second.refs_2_), channel_id=1, source_target_pairs={{0,1},{1,0},{2,3},{3,2},{4,5},{5,4},{6,7},{7,6},{8,9},{9,8},{10,11... | collective-permute-start | bytes 983048 | tf_op jit(solution)/shard_map/ppermute | solution.py:21
  46.1 6.6 %collective-permute-start.8 = (bf16[4,80,256]{2,1,0:T(8,128)(2,1)S(1)}, bf16[4,80,256]{2,1,0:T(8,128)(2,1)S(1)}, u32[]{:S(2)}, u32[]{:S(2)}) collective-permute-start(bf16[4,80,256]{2,1,0:T(8,128)(2,1)S(1)} %collective-permute-done.2.refs_3_), channel_id=1, source_target_pairs={{0,8},{8,128},{128,136},{136,0},{1,9},{9,129},{129,137},{137,1},{2... | collective-permute-start | bytes 491528 | tf_op jit(solution)/shard_map/ppermute | solution.py:21
  46.5 7.5 %collective-permute-start.9 = (bf16[4,80,256]{2,1,0:T(8,128)(2,1)S(1)}, bf16[4,80,256]{2,1,0:T(8,128)(2,1)S(1)}, u32[]{:S(2)}, u32[]{:S(2)}) collective-permute-start(bf16[4,80,256]{2,1,0:T(8,128)(2,1)S(1)} %collective-permute-done.3.refs_4_), channel_id=1, source_target_pairs={{0,136},{8,0},{128,8},{136,128},{1,137},{9,1},{129,9},{137,129},{2... | collective-permute-start | bytes 491528 | tf_op jit(solution)/shard_map/ppermute | solution.py:21
  48.8 5.8 %collective-permute-start.13 = (bf16[4,80,256]{2,1,0:T(8,128)(2,1)S(1)}, bf16[4,80,256]{2,1,0:T(8,128)(2,1)S(1)}, u32[]{:S(2)}, u32[]{:S(2)}) collective-permute-start(bf16[4,80,256]{2,1,0:T(8,128)(2,1)S(1)} %collective-permute-done.2.refs_3_), channel_id=1, source_target_pairs={{0,1},{1,0},{2,3},{3,2},{4,5},{5,4},{6,7},{7,6},{8,9},{9,8},{10,11... | collective-permute-start | bytes 491528 | tf_op jit(solution)/shard_map/ppermute | solution.py:21
  52.7 3.6 %collective-permute-start.17 = (bf16[8,80,256]{2,1,0:T(8,128)(2,1)S(1)}, bf16[8,80,256]{2,1,0:T(8,128)(2,1)S(1)}, u32[]{:S(2)}, u32[]{:S(2)}) collective-permute-start(bf16[8,80,256]{2,1,0:T(8,128)(2,1)S(1)} %collective-permute-done.4.refs_7_), channel_id=1, source_target_pairs={{0,1},{1,0},{2,3},{3,2},{4,5},{5,4},{6,7},{7,6},{8,9},{9,8},{10,11... | collective-permute-start | bytes 983048 | tf_op jit(solution)/shard_map/ppermute | solution.py:21
  53.9 2.4 %collective-permute-start.18 = (bf16[8,80,256]{2,1,0:T(8,128)(2,1)S(1)}, bf16[8,80,256]{2,1,0:T(8,128)(2,1)S(1)}, u32[]{:S(2)}, u32[]{:S(2)}) collective-permute-start(bf16[8,80,256]{2,1,0:T(8,128)(2,1)S(1)} %collective-permute-done.5.refs_8_), channel_id=1, source_target_pairs={{0,1},{1,0},{2,3},{3,2},{4,5},{5,4},{6,7},{7,6},{8,9},{9,8},{10,11... | collective-permute-start | bytes 983048 | tf_op jit(solution)/shard_map/ppermute | solution.py:21
  59.1 5.5 %collective-permute-start.21 = (bf16[80,1024]{1,0:T(8,128)(2,1)S(1)}, bf16[80,1024]{1,0:T(8,128)(2,1)S(1)}, u32[]{:S(2)}, u32[]{:S(2)}) collective-permute-start(bf16[80,1024]{1,0:T(8,128)(2,1)S(1)} %shard_map.30.refs_0_), channel_id=1, source_target_pairs={{0,8},{8,0},{1,9},{9,1},{2,10},{10,2},{3,11},{11,3},{4,12},{12,4},... | collective-permute-start | bytes 491528 | tf_op jit(solution)/shard_map/ppermute | solution.py:21
  59.2 8.0 %collective-permute-start.25 = (bf16[80,1024]{1,0:T(8,128)(2,1)S(1)}, bf16[80,1024]{1,0:T(8,128)(2,1)S(1)}, u32[]{:S(2)}, u32[]{:S(2)}) collective-permute-start(bf16[80,1024]{1,0:T(8,128)(2,1)S(1)} %shard_map.30.refs_0_), channel_id=1, source_target_pairs={{0,112},{16,0},{32,16},{48,32},{64,48},{80,64},{96,80},{112,96},{1... | collective-permute-start | bytes 491528 | tf_op jit(solution)/shard_map/ppermute | solution.py:21
  59.3 7.9 %collective-permute-start.22 = (bf16[80,1024]{1,0:T(8,128)(2,1)S(1)}, bf16[80,1024]{1,0:T(8,128)(2,1)S(1)}, u32[]{:S(2)}, u32[]{:S(2)}) collective-permute-start(bf16[80,1024]{1,0:T(8,128)(2,1)S(1)} %shard_map.30.refs_0_), channel_id=1, source_target_pairs={{0,16},{16,32},{32,48},{48,64},{64,80},{80,96},{96,112},{112,0},{1... | collective-permute-start | bytes 491528 | tf_op jit(solution)/shard_map/ppermute | solution.py:21
  64.6 8.5 %collective-permute-start.29 = (bf16[2,80,1024]{2,1,0:T(8,128)(2,1)S(1)}, bf16[2,80,1024]{2,1,0:T(8,128)(2,1)S(1)}, u32[]{:S(2)}, u32[]{:S(2)}) collective-permute-start(bf16[2,80,1024]{2,1,0:T(8,128)(2,1)S(1)} %shard_map.31.near), channel_id=1, source_target_pairs={{0,6},{2,0},{4,2},{6,4},{1,7},{3,1},{5,3},{7,5},{8,14},{10,8},{12,... | collective-permute-start | bytes 983048 | tf_op jit(solution)/shard_map/ppermute | solution.py:21
  67.2 8.9 %collective-permute-start.28 = (bf16[2,80,1024]{2,1,0:T(8,128)(2,1)S(1)}, bf16[2,80,1024]{2,1,0:T(8,128)(2,1)S(1)}, u32[]{:S(2)}, u32[]{:S(2)}) collective-permute-start(bf16[2,80,1024]{2,1,0:T(8,128)(2,1)S(1)} %shard_map.31.near), channel_id=1, source_target_pairs={{0,2},{2,4},{4,6},{6,0},{1,3},{3,5},{5,7},{7,1},{8,10},{10,12},{12... | collective-permute-start | bytes 983048 | tf_op jit(solution)/shard_map/ppermute | solution.py:21
  67.2 4.5 %collective-permute-start.26 = (bf16[80,1024]{1,0:T(8,128)(2,1)S(1)}, bf16[80,1024]{1,0:T(8,128)(2,1)S(1)}, u32[]{:S(2)}, u32[]{:S(2)}) collective-permute-start(bf16[80,1024]{1,0:T(8,128)(2,1)S(1)} %collective-permute-done.25.refs_2_), channel_id=1, source_target_pairs={{0,112},{16,0},{32,16},{48,32},{64,48},{80,64},{96,80},{112,96},{1... | collective-permute-start | bytes 491528 | tf_op jit(solution)/shard_map/ppermute | solution.py:21
  67.2 5.7 %collective-permute-start.23 = (bf16[80,1024]{1,0:T(8,128)(2,1)S(1)}, bf16[80,1024]{1,0:T(8,128)(2,1)S(1)}, u32[]{:S(2)}, u32[]{:S(2)}) collective-permute-start(bf16[80,1024]{1,0:T(8,128)(2,1)S(1)} %collective-permute-done.22.refs_1_), channel_id=1, source_target_pairs={{0,16},{16,32},{32,48},{48,64},{64,80},{80,96},{96,112},{112,0},{1... | collective-permute-start | bytes 491528 | tf_op jit(solution)/shard_map/ppermute | solution.py:21
  71.7 4.5 %collective-permute-start.27 = (bf16[80,1024]{1,0:T(8,128)(2,1)S(1)}, bf16[80,1024]{1,0:T(8,128)(2,1)S(1)}, u32[]{:S(2)}, u32[]{:S(2)}) collective-permute-start(bf16[80,1024]{1,0:T(8,128)(2,1)S(1)} %collective-permute-done.26.refs_4_), channel_id=1, source_target_pairs={{0,112},{16,0},{32,16},{48,32},{64,48},{80,64},{96,80},{112,96},{1... | collective-permute-start | bytes 491528 | tf_op jit(solution)/shard_map/ppermute | solution.py:21
  72.9 5.4 %collective-permute-start.24 = (bf16[80,1024]{1,0:T(8,128)(2,1)S(1)}, bf16[80,1024]{1,0:T(8,128)(2,1)S(1)}, u32[]{:S(2)}, u32[]{:S(2)}) collective-permute-start(bf16[80,1024]{1,0:T(8,128)(2,1)S(1)} %collective-permute-done.23.refs_3_), channel_id=1, source_target_pairs={{0,16},{16,32},{32,48},{48,64},{64,80},{80,96},{96,112},{112,0},{1... | collective-permute-start | bytes 491528 | tf_op jit(solution)/shard_map/ppermute | solution.py:21
  78.3 7.2 %collective-permute-start.30 = (bf16[80,1024]{1,0:T(8,128)(2,1)S(1)}, bf16[80,1024]{1,0:T(8,128)(2,1)S(1)}, u32[]{:S(2)}, u32[]{:S(2)}) collective-permute-start(bf16[80,1024]{1,0:T(8,128)(2,1)S(1)} %collective-permute-done.24.refs_5_), channel_id=1, source_target_pairs={{0,16},{16,32},{32,48},{48,64},{64,80},{80,96},{96,112},{112,0},{1... | collective-permute-start | bytes 491528 | tf_op jit(solution)/shard_map/ppermute | solution.py:21
  78.3 10.1 %collective-permute-start.31 = (bf16[1,80,1024]{2,1,0:T(8,128)(2,1)S(1)}, bf16[1,80,1024]{2,1,0:T(8,128)(2,1)S(1)}, u32[]{:S(2)}, u32[]{:S(2)}) collective-permute-start(bf16[1,80,1024]{2,1,0:T(8,128)(2,1)S(1)} %get-tuple-element.45), channel_id=1, source_target_pairs={{0,2},{2,4},{4,6},{6,0},{1,3},{3,5},{5,7},{7,1},{8,10},{10,12},{12... | collective-permute-start | bytes 491528 | tf_op jit(solution)/shard_map/ppermute | solution.py:21
  78.4 10.1 %collective-permute-start.32 = (bf16[1,80,1024]{2,1,0:T(8,128)(2,1)S(1)}, bf16[1,80,1024]{2,1,0:T(8,128)(2,1)S(1)}, u32[]{:S(2)}, u32[]{:S(2)}) collective-permute-start(bf16[1,80,1024]{2,1,0:T(8,128)(2,1)S(1)} %get-tuple-element.46), channel_id=1, source_target_pairs={{0,6},{2,0},{4,2},{6,4},{1,7},{3,1},{5,3},{7,5},{8,14},{10,8},{12,... | collective-permute-start | bytes 491528 | tf_op jit(solution)/shard_map/ppermute | solution.py:21
  81.4 7.5 %collective-permute-start.33 = (bf16[80,1024]{1,0:T(8,128)(2,1)S(1)}, bf16[80,1024]{1,0:T(8,128)(2,1)S(1)}, u32[]{:S(2)}, u32[]{:S(2)}) collective-permute-start(bf16[80,1024]{1,0:T(8,128)(2,1)S(1)} %shard_map.30.refs_0_), channel_id=1, source_target_pairs={{0,1},{1,0},{2,3},{3,2},{4,5},{5,4},{6,7},{7,6},{8,9},{9,8},{10,11... | collective-permute-start | bytes 491528 | tf_op jit(solution)/shard_map/ppermute | solution.py:21
  85.5 3.5 %collective-permute-start.35 = (bf16[80,1024]{1,0:T(8,128)(2,1)S(1)}, bf16[80,1024]{1,0:T(8,128)(2,1)S(1)}, u32[]{:S(2)}, u32[]{:S(2)}) collective-permute-start(bf16[80,1024]{1,0:T(8,128)(2,1)S(1)} %collective-permute-done.25.refs_2_), channel_id=1, source_target_pairs={{0,1},{1,0},{2,3},{3,2},{4,5},{5,4},{6,7},{7,6},{8,9},{9,8},{10,11... | collective-permute-start | bytes 491528 | tf_op jit(solution)/shard_map/ppermute | solution.py:21
  85.5 3.9 %collective-permute-start.34 = (bf16[80,1024]{1,0:T(8,128)(2,1)S(1)}, bf16[80,1024]{1,0:T(8,128)(2,1)S(1)}, u32[]{:S(2)}, u32[]{:S(2)}) collective-permute-start(bf16[80,1024]{1,0:T(8,128)(2,1)S(1)} %collective-permute-done.22.refs_1_), channel_id=1, source_target_pairs={{0,1},{1,0},{2,3},{3,2},{4,5},{5,4},{6,7},{7,6},{8,9},{9,8},{10,11... | collective-permute-start | bytes 491528 | tf_op jit(solution)/shard_map/ppermute | solution.py:21
  (11 other events, 46.8 us)

commit v3 on v2

--- a/solution.py
+++ b/solution.py
@@ -23,6 +23,11 @@
 
 def swap(value):
     return shift(value, "c", 1)
+
+
+def cross(value):
+    steps = [(zi * 2 + ci, (zi - 1) % 8 * 2 + 1 - ci) for zi in range(8) for ci in range(2)]
+    return lax.ppermute(value, ("z", "c"), steps)
 
 
 def together(*values):
@@ -109,13 +114,15 @@
     return call(stack_kernel, [(len(values),) + values[0].shape], [(VMEM, v) for v in values], 4)[0]
 
 
-def product_kernel(where, near, left, right, far0, far1, *refs):
+def product_kernel(where, near, left, right, far, yfar, *refs):
     cols, (out, lefts, rights) = refs[:16], refs[16:]
     yl, z, x, c = (where[i] for i in range(1, 5))
-    for ref, along_x, first in ((near, 0, 0), (left, 3, 0), (right, 1, 0), (far0, 2, 0), (far1, 2, 1)):
-        for i in range(ref.shape[0]):
-            side = 1 - yl if first + i else yl
+    for ref, along_x in ((near, 0), (left, 3), (right, 1)):
+        for i in range(2):
+            side = 1 - yl if i else yl
             lefts[side * 4 + lax.rem(x + along_x, 4)] = ref[i]
+    lefts[yl * 4 + lax.rem(x + 2, 4)] = far[...]
+    lefts[(1 - yl) * 4 + lax.rem(x + 2, 4)] = yfar[...]
     for other in range(2):
         core = 1 - c if other else c
         for ref, along in zip(cols[other * 8:other * 8 + 8], RING8):
@@ -188,17 +195,15 @@
     up, down = shift(unit, "z", 1), shift(unit, "z", -1)
     near = stack(unit, ynear)
     left, right = shift(near, "x", 1), shift(near, "x", -1)
+    far = shift(unit, "x", 2)
+    yfar = shift(far, "yl", 1)
     up2, down2 = shift(up, "z", 1), shift(down, "z", -1)
     up3, down3 = shift(up2, "z", 1), shift(down2, "z", -1)
-    up3, down3, left, right = together(up3, down3, left, right)
-    far = cut(left, right)
-    far = [shift(far[0], "x", 1), shift(far[1], "x", -1)]
-    up4 = shift(up3, "z", 1)
-    up4, *far = together(up4, *far)
-    cols = [unit, up, down, up2, down2, up3, down3, up4]
-    cols += [swap(v) for v in cols]
-
-    block = product(where, [near, left, right, *far], cols)
+    up3, down3, left, right, far, yfar = together(up3, down3, left, right, far, yfar)
+    cols = [unit, up, down, up2, down2, up3, down3]
+    cols += [shift(up3, "z", 1), *(swap(v) for v in cols), cross(down3)]
+
+    block = product(where, [near, left, right, far, yfar], cols)
     return spread(lax.all_to_all(block, ("yh", "yl", "x"), split_axis=0, concat_axis=0, tiled=True))
 
 

time: 124 us -> 123 us (level)
  waiting for transfers between devices: 20 us -> 16.8 us
  starting transfers between devices: 43.6 us -> 45.3 us
    ppermute x41 -> x40, waiting for transfers between devices: 20 us -> 16 us  [shift(): lax.ppermute(value, axis, [(i, (i + by) % count) for i in range(count)])]
    ppermute x0 -> x1, starting transfers between devices: none -> 3.25 us  [cross(): return lax.ppermute(value, ('z', 'c'), steps)]
    ppermute x41 -> x40, starting transfers between devices: 43.6 us -> 42 us  [shift(): lax.ppermute(value, axis, [(i, (i + by) % count) for i in range(count)])]
    pallas_call x6 -> x5, Pallas kernels: 5.49 us -> 5.47 us  [call(): pl.pallas_call(kernel, out_shape=shapes, in_specs=[spec for spec, _ in in...]
  transfers between devices with their start and end apart: 41 -> 41, of which waited for: 14 -> 11; matrix products, arithmetic and copies ran while one was open for 0% -> 0% of each run, Pallas kernels for 0% -> 0%
where the time goes in v3:
time: 123 us; the launch traced here: 122 us
  blocking collectives  49.1 us (40%)
  starting transfers between devices  45.3 us (37%)
  waiting for transfers between devices  16.8 us (14%)
  Pallas kernels  7.21 us (6%)
  local copies, waits for them, and re-layouts  3.75 us (3%)
    ppermute x40, starting transfers between devices, shift(): lax.ppermute(value, axis, [(i, (i + by) % count) for i in range(count)])  42 us
    all_to_all x1, blocking collectives, per_device(): lax.all_to_all(block, ('yh', 'yl', 'x'), split_axis=0, concat_axis=0, til...  28.6 us
    all_to_all x1, blocking collectives, everywhere(): return lax.all_to_all(copies, axes, split_axis=0, concat_axis=0, tiled=True)  20.5 us
    ppermute x40, waiting for transfers between devices, shift(): lax.ppermute(value, axis, [(i, (i + by) % count) for i in range(count)])  16 us
    pallas_call x5, Pallas kernels, call(): pl.pallas_call(kernel, out_shape=shapes, in_specs=[spec for spec, _ in in...  5.47 us
    ppermute x1, starting transfers between devices, cross(): return lax.ppermute(value, ('z', 'c'), steps)  3.25 us
    unnamed x4, local copies, waits for them, and re-layouts  2.86 us
  transfers between devices with their start and end apart: 41, of which 11 were waited for; matrix products, arithmetic and copies ran while one was open for 0% of the time, Pallas kernels for 0%

profile of v3, /device:TPU:1, one launch (start us, length us, event | category | flops | bytes accessed | tf_op | source)
XLA Modules:
  0.0 122.2 jit_solution(14177061080939466601)
XLA Ops:
  0.1 0.8 broadcast_in_dim.2
  0.9 20.5 %all_to_all.10.first.second.refs_0_ = bf16[8,80,256]{2,1,0:T(8,128)(2,1)S(1)} all-to-all(bf16[8,80,256]{2,1,0:T(8,128)(2,1)S(1)} %broadcast_in_dim.2), channel_id=1, replica_groups=mesh['yh'=2,'z'=8,'yl'=2,'x'=4,'c'=2] {'z'}, dimensions={0} | all-to-all | bytes 655360 | tf_op jit(solution)/shard_map/all_to_all | solution.py:53
  21.4 2.5 %collective-permute-start.1 = (bf16[8,80,256]{2,1,0:T(8,128)(2,1)S(1)}, bf16[8,80,256]{2,1,0:T(8,128)(2,1)S(1)}, u32[]{:S(2)}, u32[]{:S(2)}) collective-permute-start(bf16[8,80,256]{2,1,0:T(8,128)(2,1)S(1)} %all_to_all.10.first.second.refs_0_), channel_id=1, source_target_pairs={{0,6},{2,0},{4,2},{6,4},{1,7},{3,1},{5,3},{7,5},{8,14},{10,8},{12,... | collective-permute-start | bytes 983048 | tf_op jit(solution)/shard_map/ppermute | solution.py:21
  23.9 2.9 %copy-done = bf16[4,80,10240]{2,1,0:T(8,128)(2,1)S(1)} copy-done((bf16[4,80,10240]{2,1,0:T(8,128)(2,1)S(1)}, bf16[4,80,10240]{2,1,0:T(8,128)(2,1)}, u32[]{:S(2)}) %copy-start) | copy-done | bytes 6553624
  26.7 1.4 %collective-permute-start.6 = (bf16[4,80,256]{2,1,0:T(8,128)(2,1)S(1)}, bf16[4,80,256]{2,1,0:T(8,128)(2,1)S(1)}, u32[]{:S(2)}, u32[]{:S(2)}) collective-permute-start(bf16[4,80,256]{2,1,0:T(8,128)(2,1)S(1)} %get-tuple-element.33), channel_id=1, source_target_pairs={{0,8},{8,128},{128,136},{136,0},{1,9},{9,129},{129,137},{137,1},{2... | collective-permute-start | bytes 491528 | tf_op jit(solution)/shard_map/ppermute | solution.py:21
  28.1 1.5 %collective-permute-start.7 = (bf16[4,80,256]{2,1,0:T(8,128)(2,1)S(1)}, bf16[4,80,256]{2,1,0:T(8,128)(2,1)S(1)}, u32[]{:S(2)}, u32[]{:S(2)}) collective-permute-start(bf16[4,80,256]{2,1,0:T(8,128)(2,1)S(1)} %get-tuple-element.34), channel_id=1, source_target_pairs={{0,136},{8,0},{128,8},{136,128},{1,137},{9,1},{129,9},{137,129},{2... | collective-permute-start | bytes 491528 | tf_op jit(solution)/shard_map/ppermute | solution.py:21
  29.6 1.8 %collective-permute-done.first.refs_1_ = bf16[8,80,256]{2,1,0:T(8,128)(2,1)S(1)} collective-permute-done((bf16[8,80,256]{2,1,0:T(8,128)(2,1)S(1)}, bf16[8,80,256]{2,1,0:T(8,128)(2,1)S(1)}, u32[]{:S(2)}, u32[]{:S(2)}) %collective-permute-start) | collective-permute-done | bytes 327712 | tf_op jit(solution)/shard_map/ppermute | solution.py:21
  31.4 1.3 %collective-permute-start.4 = (bf16[8,80,256]{2,1,0:T(8,128)(2,1)S(1)}, bf16[8,80,256]{2,1,0:T(8,128)(2,1)S(1)}, u32[]{:S(2)}, u32[]{:S(2)}) collective-permute-start(bf16[8,80,256]{2,1,0:T(8,128)(2,1)S(1)} %collective-permute-done.first.refs_1_), channel_id=1, source_target_pairs={{0,8},{8,128},{128,136},{136,0},{1,9},{9,129},{129,137},{137,1},{2... | collective-permute-start | bytes 983048 | tf_op jit(solution)/shard_map/ppermute | solution.py:21
  32.7 1.4 %collective-permute-start.5 = (bf16[8,80,256]{2,1,0:T(8,128)(2,1)S(1)}, bf16[8,80,256]{2,1,0:T(8,128)(2,1)S(1)}, u32[]{:S(2)}, u32[]{:S(2)}) collective-permute-start(bf16[8,80,256]{2,1,0:T(8,128)(2,1)S(1)} %collective-permute-done.1.second.refs_2_), channel_id=1, source_target_pairs={{0,136},{8,0},{128,8},{136,128},{1,137},{9,1},{129,9},{137,129},{2... | collective-permute-start | bytes 983048 | tf_op jit(solution)/shard_map/ppermute | solution.py:21
  34.3 2.7 %collective-permute-start.3 = (bf16[4,80,256]{2,1,0:T(8,128)(2,1)S(1)}, bf16[4,80,256]{2,1,0:T(8,128)(2,1)S(1)}, u32[]{:S(2)}, u32[]{:S(2)}) collective-permute-start(bf16[4,80,256]{2,1,0:T(8,128)(2,1)S(1)} %get-tuple-element.30), channel_id=1, source_target_pairs={{0,6},{2,0},{4,2},{6,4},{1,7},{3,1},{5,3},{7,5},{8,14},{10,8},{12,... | collective-permute-start | bytes 491528 | tf_op jit(solution)/shard_map/ppermute | solution.py:21
  36.9 4.8 %collective-permute-start.10 = (bf16[8,80,256]{2,1,0:T(8,128)(2,1)S(1)}, bf16[8,80,256]{2,1,0:T(8,128)(2,1)S(1)}, u32[]{:S(2)}, u32[]{:S(2)}) collective-permute-start(bf16[8,80,256]{2,1,0:T(8,128)(2,1)S(1)} %all_to_all.10.first.second.refs_0_), channel_id=1, source_target_pairs={{0,1},{1,0},{2,3},{3,2},{4,5},{5,4},{6,7},{7,6},{8,9},{9,8},{10,11... | collective-permute-start | bytes 983048 | tf_op jit(solution)/shard_map/ppermute | solution.py:21
  41.8 3.3 %collective-permute-start.15 = (bf16[4,80,256]{2,1,0:T(8,128)(2,1)S(1)}, bf16[4,80,256]{2,1,0:T(8,128)(2,1)S(1)}, u32[]{:S(2)}, u32[]{:S(2)}) collective-permute-start(bf16[4,80,256]{2,1,0:T(8,128)(2,1)S(1)} %collective-permute-done.6.refs_5_), channel_id=1, source_target_pairs={{0,1},{1,0},{2,3},{3,2},{4,5},{5,4},{6,7},{7,6},{8,9},{9,8},{10,11... | collective-permute-start | bytes 491528 | tf_op jit(solution)/shard_map/ppermute | solution.py:21
  46.5 2.3 %collective-permute-start.9 = (bf16[4,80,256]{2,1,0:T(8,128)(2,1)S(1)}, bf16[4,80,256]{2,1,0:T(8,128)(2,1)S(1)}, u32[]{:S(2)}, u32[]{:S(2)}) collective-permute-start(bf16[4,80,256]{2,1,0:T(8,128)(2,1)S(1)} %collective-permute-done.3.refs_4_), channel_id=1, source_target_pairs={{0,136},{8,0},{128,8},{136,128},{1,137},{9,1},{129,9},{137,129},{2... | collective-permute-start | bytes 491528 | tf_op jit(solution)/shard_map/ppermute | solution.py:21
  48.8 0.9 collective-permute-start.13
  49.7 3.0 %collective-permute-done.8.refs_9_ = bf16[4,80,256]{2,1,0:T(8,128)(2,1)S(1)} collective-permute-done((bf16[4,80,256]{2,1,0:T(8,128)(2,1)S(1)}, bf16[4,80,256]{2,1,0:T(8,128)(2,1)S(1)}, u32[]{:S(2)}, u32[]{:S(2)}) %collective-permute-start.8) | collective-permute-done | bytes 163872 | tf_op jit(solution)/shard_map/ppermute | solution.py:21
  52.7 1.2 collective-permute-start.17
  55.0 0.9 collective-permute-done.14.refs_15_
  56.4 2.8 %shard_map.30.refs_0_ = bf16[80,1024]{1,0:T(8,128)(2,1)S(1)} custom-call(s32[5]{0:T(128)S(1)} %stack.23.where, bf16[320,10240]{1,0:T(8,128)(2,1)S(1)} %bitcast.7, bf16[8,80,256]{2,1,0:T(8,128)(2,1)S(1)} %all_to_all.10.first.second.refs_0_, bf16[8,80,256]{2,1,0:T(8,128)(2,1)S(1)} %collective-permute-done.first.refs_1_, ...), custom_call_target="tpu_custom_call" | custom-call | flops 1677721600 | bytes 12582912 | tf_op jit(solution)/shard_map/pallas_call | solution.py:39
  59.3 1.5 %collective-permute-start.22 = (bf16[80,1024]{1,0:T(8,128)(2,1)S(1)}, bf16[80,1024]{1,0:T(8,128)(2,1)S(1)}, u32[]{:S(2)}, u32[]{:S(2)}) collective-permute-start(bf16[80,1024]{1,0:T(8,128)(2,1)S(1)} %shard_map.30.refs_0_), channel_id=1, source_target_pairs={{0,16},{16,32},{32,48},{48,64},{64,80},{80,96},{96,112},{112,0},{1... | collective-permute-start | bytes 491528 | tf_op jit(solution)/shard_map/ppermute | solution.py:21
  61.5 3.2 %collective-permute-done.21.refs_1_ = bf16[80,1024]{1,0:T(8,128)(2,1)S(1)} collective-permute-done((bf16[80,1024]{1,0:T(8,128)(2,1)S(1)}, bf16[80,1024]{1,0:T(8,128)(2,1)S(1)}, u32[]{:S(2)}, u32[]{:S(2)}) %collective-permute-start.21) | collective-permute-done | bytes 163872 | tf_op jit(solution)/shard_map/ppermute | solution.py:21
  64.6 2.5 %collective-permute-start.29 = (bf16[2,80,1024]{2,1,0:T(8,128)(2,1)S(1)}, bf16[2,80,1024]{2,1,0:T(8,128)(2,1)S(1)}, u32[]{:S(2)}, u32[]{:S(2)}) collective-permute-start(bf16[2,80,1024]{2,1,0:T(8,128)(2,1)S(1)} %shard_map.31.near), channel_id=1, source_target_pairs={{0,6},{2,0},{4,2},{6,4},{1,7},{3,1},{5,3},{7,5},{8,14},{10,8},{12,... | collective-permute-start | bytes 983048 | tf_op jit(solution)/shard_map/ppermute | solution.py:21
  67.2 1.5 %collective-permute-start.23 = (bf16[80,1024]{1,0:T(8,128)(2,1)S(1)}, bf16[80,1024]{1,0:T(8,128)(2,1)S(1)}, u32[]{:S(2)}, u32[]{:S(2)}) collective-permute-start(bf16[80,1024]{1,0:T(8,128)(2,1)S(1)} %collective-permute-done.22.refs_1_), channel_id=1, source_target_pairs={{0,16},{16,32},{32,48},{48,64},{64,80},{80,96},{96,112},{112,0},{1... | collective-permute-start | bytes 491528 | tf_op jit(solution)/shard_map/ppermute | solution.py:21
  69.0 2.7 %collective-permute-done.26.refs_4_ = bf16[80,1024]{1,0:T(8,128)(2,1)S(1)} collective-permute-done((bf16[80,1024]{1,0:T(8,128)(2,1)S(1)}, bf16[80,1024]{1,0:T(8,128)(2,1)S(1)}, u32[]{:S(2)}, u32[]{:S(2)}) %collective-permute-start.26) | collective-permute-done | bytes 163872 | tf_op jit(solution)/shard_map/ppermute | solution.py:21
  71.7 1.2 %collective-permute-start.27 = (bf16[80,1024]{1,0:T(8,128)(2,1)S(1)}, bf16[80,1024]{1,0:T(8,128)(2,1)S(1)}, u32[]{:S(2)}, u32[]{:S(2)}) collective-permute-start(bf16[80,1024]{1,0:T(8,128)(2,1)S(1)} %collective-permute-done.26.refs_4_), channel_id=1, source_target_pairs={{0,112},{16,0},{32,16},{48,32},{64,48},{80,64},{96,80},{112,96},{1... | collective-permute-start | bytes 491528 | tf_op jit(solution)/shard_map/ppermute | solution.py:21
  73.1 2.9 %collective-permute-start.33 = (bf16[80,1024]{1,0:T(8,128)(2,1)S(1)}, bf16[80,1024]{1,0:T(8,128)(2,1)S(1)}, u32[]{:S(2)}, u32[]{:S(2)}) collective-permute-start(bf16[80,1024]{1,0:T(8,128)(2,1)S(1)} %shard_map.30.refs_0_), channel_id=1, source_target_pairs={{0,1},{1,0},{2,3},{3,2},{4,5},{5,4},{6,7},{7,6},{8,9},{9,8},{10,11... | collective-permute-start | bytes 491528 | tf_op jit(solution)/shard_map/ppermute | solution.py:21
  76.1 2.4 %collective-permute-start.34 = (bf16[80,1024]{1,0:T(8,128)(2,1)S(1)}, bf16[80,1024]{1,0:T(8,128)(2,1)S(1)}, u32[]{:S(2)}, u32[]{:S(2)}) collective-permute-start(bf16[80,1024]{1,0:T(8,128)(2,1)S(1)} %collective-permute-done.22.refs_1_), channel_id=1, source_target_pairs={{0,1},{1,0},{2,3},{3,2},{4,5},{5,4},{6,7},{7,6},{8,9},{9,8},{10,11... | collective-permute-start | bytes 491528 | tf_op jit(solution)/shard_map/ppermute | solution.py:21
  79.3 2.5 %collective-permute-start.36 = (bf16[80,1024]{1,0:T(8,128)(2,1)S(1)}, bf16[80,1024]{1,0:T(8,128)(2,1)S(1)}, u32[]{:S(2)}, u32[]{:S(2)}) collective-permute-start(bf16[80,1024]{1,0:T(8,128)(2,1)S(1)} %collective-permute-done.23.refs_3_), channel_id=1, source_target_pairs={{0,1},{1,0},{2,3},{3,2},{4,5},{5,4},{6,7},{7,6},{8,9},{9,8},{10,11... | collective-permute-start | bytes 491528 | tf_op jit(solution)/shard_map/ppermute | solution.py:21
  82.0 3.2 %collective-permute-start.40 = (bf16[80,1024]{1,0:T(8,128)(2,1)S(1)}, bf16[80,1024]{1,0:T(8,128)(2,1)S(1)}, u32[]{:S(2)}, u32[]{:S(2)}) collective-permute-start(bf16[80,1024]{1,0:T(8,128)(2,1)S(1)} %collective-permute-done.27.refs_6_), channel_id=1, source_target_pairs={{0,113},{1,112},{16,1},{17,0},{32,17},{33,16},{48,33},{49,32},{64,... | collective-permute-start | bytes 491528 | tf_op jit(solution)/shard_map/ppermute | solution.py:30
  85.2 3.3 %collective-permute-done.32.refs_7_ = bf16[80,1024]{1,0:T(8,128)(2,1)S(1)} collective-permute-done((bf16[80,1024]{1,0:T(8,128)(2,1)S(1)}, bf16[80,1024]{1,0:T(8,128)(2,1)S(1)}, u32[]{:S(2)}, u32[]{:S(2)}) %collective-permute-start.32) | collective-permute-done | bytes 163872 | tf_op jit(solution)/shard_map/ppermute | solution.py:21
  89.2 2.6 %shard_map.32 = bf16[16,80,640]{2,1,0:T(8,128)(2,1)S(1)} custom-call(s32[5]{0:T(128)S(1)} %stack.23.where, bf16[2,80,1024]{2,1,0:T(8,128)(2,1)S(1)} %shard_map.31.near, bf16[2,80,1024]{2,1,0:T(8,128)(2,1)S(1)} %collective-permute-done.28.left, bf16[2,80,1024]{2,1,0:T(8,128)(2,1)S(1)} %collective-permute-done.29.right, ...), custom_call_target="tpu_custom_call" | custom-call | flops 1677721600 | bytes 6291456 | tf_op jit(solution)/shard_map/pallas_call | solution.py:39
  91.9 28.6 %all_to_all.11.pieces = bf16[16,80,640]{2,1,0:T(8,128)(2,1)S(1)} all-to-all(bf16[16,80,640]{2,1,0:T(8,128)(2,1)S(1)} %shard_map.32), channel_id=1, replica_groups=mesh['yh'=2,'z'=8,'yl'=2,'x'=4,'c'=2] {'yh','yl','x'}, dimensions={0} | all-to-all | bytes 3276800 | tf_op jit(solution)/shard_map/all_to_all | solution.py:207
  120.5 1.7 %shard_map.33 = f32[80,5120]{1,0:T(8,128)} custom-call(bf16[16,80,640]{2,1,0:T(8,128)(2,1)S(1)} %all_to_all.11.pieces), custom_call_target="tpu_custom_call" | custom-call | bytes 4194304 | tf_op jit(solution)/shard_map/pallas_call | solution.py:161
  (64 shorter events, 6.3 us)
Async XLA Ops:
  21.4 8.3 %collective-permute-start.1 = (bf16[8,80,256]{2,1,0:T(8,128)(2,1)S(1)}, bf16[8,80,256]{2,1,0:T(8,128)(2,1)S(1)}, u32[]{:S(2)}, u32[]{:S(2)}) collective-permute-start(bf16[8,80,256]{2,1,0:T(8,128)(2,1)S(1)} %all_to_all.10.first.second.refs_0_), channel_id=1, source_target_pairs={{0,6},{2,0},{4,2},{6,4},{1,7},{3,1},{5,3},{7,5},{8,14},{10,8},{12,... | collective-permute-start | bytes 983048 | tf_op jit(solution)/shard_map/ppermute | solution.py:21
  23.9 7.6 %collective-permute-start = (bf16[8,80,256]{2,1,0:T(8,128)(2,1)S(1)}, bf16[8,80,256]{2,1,0:T(8,128)(2,1)S(1)}, u32[]{:S(2)}, u32[]{:S(2)}) collective-permute-start(bf16[8,80,256]{2,1,0:T(8,128)(2,1)S(1)} %all_to_all.10.first.second.refs_0_), channel_id=1, source_target_pairs={{0,2},{2,4},{4,6},{6,0},{1,3},{3,5},{5,7},{7,1},{8,10},{10,12},{12... | collective-permute-start | bytes 983048 | tf_op jit(solution)/shard_map/ppermute | solution.py:21
  26.7 7.5 %collective-permute-start.6 = (bf16[4,80,256]{2,1,0:T(8,128)(2,1)S(1)}, bf16[4,80,256]{2,1,0:T(8,128)(2,1)S(1)}, u32[]{:S(2)}, u32[]{:S(2)}) collective-permute-start(bf16[4,80,256]{2,1,0:T(8,128)(2,1)S(1)} %get-tuple-element.33), channel_id=1, source_target_pairs={{0,8},{8,128},{128,136},{136,0},{1,9},{9,129},{129,137},{137,1},{2... | collective-permute-start | bytes 491528 | tf_op jit(solution)/shard_map/ppermute | solution.py:21
  28.1 8.8 %collective-permute-start.7 = (bf16[4,80,256]{2,1,0:T(8,128)(2,1)S(1)}, bf16[4,80,256]{2,1,0:T(8,128)(2,1)S(1)}, u32[]{:S(2)}, u32[]{:S(2)}) collective-permute-start(bf16[4,80,256]{2,1,0:T(8,128)(2,1)S(1)} %get-tuple-element.34), channel_id=1, source_target_pairs={{0,136},{8,0},{128,8},{136,128},{1,137},{9,1},{129,9},{137,129},{2... | collective-permute-start | bytes 491528 | tf_op jit(solution)/shard_map/ppermute | solution.py:21
  31.4 13.7 %collective-permute-start.4 = (bf16[8,80,256]{2,1,0:T(8,128)(2,1)S(1)}, bf16[8,80,256]{2,1,0:T(8,128)(2,1)S(1)}, u32[]{:S(2)}, u32[]{:S(2)}) collective-permute-start(bf16[8,80,256]{2,1,0:T(8,128)(2,1)S(1)} %collective-permute-done.first.refs_1_), channel_id=1, source_target_pairs={{0,8},{8,128},{128,136},{136,0},{1,9},{9,129},{129,137},{137,1},{2... | collective-permute-start | bytes 983048 | tf_op jit(solution)/shard_map/ppermute | solution.py:21
  32.7 12.9 %collective-permute-start.5 = (bf16[8,80,256]{2,1,0:T(8,128)(2,1)S(1)}, bf16[8,80,256]{2,1,0:T(8,128)(2,1)S(1)}, u32[]{:S(2)}, u32[]{:S(2)}) collective-permute-start(bf16[8,80,256]{2,1,0:T(8,128)(2,1)S(1)} %collective-permute-done.1.second.refs_2_), channel_id=1, source_target_pairs={{0,136},{8,0},{128,8},{136,128},{1,137},{9,1},{129,9},{137,129},{2... | collective-permute-start | bytes 983048 | tf_op jit(solution)/shard_map/ppermute | solution.py:21
  34.2 7.6 %collective-permute-start.2 = (bf16[4,80,256]{2,1,0:T(8,128)(2,1)S(1)}, bf16[4,80,256]{2,1,0:T(8,128)(2,1)S(1)}, u32[]{:S(2)}, u32[]{:S(2)}) collective-permute-start(bf16[4,80,256]{2,1,0:T(8,128)(2,1)S(1)} %get-tuple-element.29), channel_id=1, source_target_pairs={{0,2},{2,4},{4,6},{6,0},{1,3},{3,5},{5,7},{7,1},{8,10},{10,12},{12... | collective-permute-start | bytes 491528 | tf_op jit(solution)/shard_map/ppermute | solution.py:21
  34.3 10.8 %collective-permute-start.3 = (bf16[4,80,256]{2,1,0:T(8,128)(2,1)S(1)}, bf16[4,80,256]{2,1,0:T(8,128)(2,1)S(1)}, u32[]{:S(2)}, u32[]{:S(2)}) collective-permute-start(bf16[4,80,256]{2,1,0:T(8,128)(2,1)S(1)} %get-tuple-element.30), channel_id=1, source_target_pairs={{0,6},{2,0},{4,2},{6,4},{1,7},{3,1},{5,3},{7,5},{8,14},{10,8},{12,... | collective-permute-start | bytes 491528 | tf_op jit(solution)/shard_map/ppermute | solution.py:21
  36.9 11.8 %collective-permute-start.10 = (bf16[8,80,256]{2,1,0:T(8,128)(2,1)S(1)}, bf16[8,80,256]{2,1,0:T(8,128)(2,1)S(1)}, u32[]{:S(2)}, u32[]{:S(2)}) collective-permute-start(bf16[8,80,256]{2,1,0:T(8,128)(2,1)S(1)} %all_to_all.10.first.second.refs_0_), channel_id=1, source_target_pairs={{0,1},{1,0},{2,3},{3,2},{4,5},{5,4},{6,7},{7,6},{8,9},{9,8},{10,11... | collective-permute-start | bytes 983048 | tf_op jit(solution)/shard_map/ppermute | solution.py:21
  45.1 8.9 %collective-permute-start.11 = (bf16[8,80,256]{2,1,0:T(8,128)(2,1)S(1)}, bf16[8,80,256]{2,1,0:T(8,128)(2,1)S(1)}, u32[]{:S(2)}, u32[]{:S(2)}) collective-permute-start(bf16[8,80,256]{2,1,0:T(8,128)(2,1)S(1)} %collective-permute-done.first.refs_1_), channel_id=1, source_target_pairs={{0,1},{1,0},{2,3},{3,2},{4,5},{5,4},{6,7},{7,6},{8,9},{9,8},{10,11... | collective-permute-start | bytes 983048 | tf_op jit(solution)/shard_map/ppermute | solution.py:21
  45.6 8.9 %collective-permute-start.12 = (bf16[8,80,256]{2,1,0:T(8,128)(2,1)S(1)}, bf16[8,80,256]{2,1,0:T(8,128)(2,1)S(1)}, u32[]{:S(2)}, u32[]{:S(2)}) collective-permute-start(bf16[8,80,256]{2,1,0:T(8,128)(2,1)S(1)} %collective-permute-done.1.second.refs_2_), channel_id=1, source_target_pairs={{0,1},{1,0},{2,3},{3,2},{4,5},{5,4},{6,7},{7,6},{8,9},{9,8},{10,11... | collective-permute-start | bytes 983048 | tf_op jit(solution)/shard_map/ppermute | solution.py:21
  46.1 6.6 %collective-permute-start.8 = (bf16[4,80,256]{2,1,0:T(8,128)(2,1)S(1)}, bf16[4,80,256]{2,1,0:T(8,128)(2,1)S(1)}, u32[]{:S(2)}, u32[]{:S(2)}) collective-permute-start(bf16[4,80,256]{2,1,0:T(8,128)(2,1)S(1)} %collective-permute-done.2.refs_3_), channel_id=1, source_target_pairs={{0,8},{8,128},{128,136},{136,0},{1,9},{9,129},{129,137},{137,1},{2... | collective-permute-start | bytes 491528 | tf_op jit(solution)/shard_map/ppermute | solution.py:21
  46.5 7.5 %collective-permute-start.9 = (bf16[4,80,256]{2,1,0:T(8,128)(2,1)S(1)}, bf16[4,80,256]{2,1,0:T(8,128)(2,1)S(1)}, u32[]{:S(2)}, u32[]{:S(2)}) collective-permute-start(bf16[4,80,256]{2,1,0:T(8,128)(2,1)S(1)} %collective-permute-done.3.refs_4_), channel_id=1, source_target_pairs={{0,136},{8,0},{128,8},{136,128},{1,137},{9,1},{129,9},{137,129},{2... | collective-permute-start | bytes 491528 | tf_op jit(solution)/shard_map/ppermute | solution.py:21
  48.8 5.8 %collective-permute-start.13 = (bf16[4,80,256]{2,1,0:T(8,128)(2,1)S(1)}, bf16[4,80,256]{2,1,0:T(8,128)(2,1)S(1)}, u32[]{:S(2)}, u32[]{:S(2)}) collective-permute-start(bf16[4,80,256]{2,1,0:T(8,128)(2,1)S(1)} %collective-permute-done.2.refs_3_), channel_id=1, source_target_pairs={{0,1},{1,0},{2,3},{3,2},{4,5},{5,4},{6,7},{7,6},{8,9},{9,8},{10,11... | collective-permute-start | bytes 491528 | tf_op jit(solution)/shard_map/ppermute | solution.py:21
  59.1 5.5 %collective-permute-start.21 = (bf16[80,1024]{1,0:T(8,128)(2,1)S(1)}, bf16[80,1024]{1,0:T(8,128)(2,1)S(1)}, u32[]{:S(2)}, u32[]{:S(2)}) collective-permute-start(bf16[80,1024]{1,0:T(8,128)(2,1)S(1)} %shard_map.30.refs_0_), channel_id=1, source_target_pairs={{0,8},{8,0},{1,9},{9,1},{2,10},{10,2},{3,11},{11,3},{4,12},{12,4},... | collective-permute-start | bytes 491528 | tf_op jit(solution)/shard_map/ppermute | solution.py:21
  59.2 8.0 %collective-permute-start.25 = (bf16[80,1024]{1,0:T(8,128)(2,1)S(1)}, bf16[80,1024]{1,0:T(8,128)(2,1)S(1)}, u32[]{:S(2)}, u32[]{:S(2)}) collective-permute-start(bf16[80,1024]{1,0:T(8,128)(2,1)S(1)} %shard_map.30.refs_0_), channel_id=1, source_target_pairs={{0,112},{16,0},{32,16},{48,32},{64,48},{80,64},{96,80},{112,96},{1... | collective-permute-start | bytes 491528 | tf_op jit(solution)/shard_map/ppermute | solution.py:21
  59.3 7.9 %collective-permute-start.22 = (bf16[80,1024]{1,0:T(8,128)(2,1)S(1)}, bf16[80,1024]{1,0:T(8,128)(2,1)S(1)}, u32[]{:S(2)}, u32[]{:S(2)}) collective-permute-start(bf16[80,1024]{1,0:T(8,128)(2,1)S(1)} %shard_map.30.refs_0_), channel_id=1, source_target_pairs={{0,16},{16,32},{32,48},{48,64},{64,80},{80,96},{96,112},{112,0},{1... | collective-permute-start | bytes 491528 | tf_op jit(solution)/shard_map/ppermute | solution.py:21
  60.8 7.9 %collective-permute-start.30 = (bf16[80,1024]{1,0:T(8,128)(2,1)S(1)}, bf16[80,1024]{1,0:T(8,128)(2,1)S(1)}, u32[]{:S(2)}, u32[]{:S(2)}) collective-permute-start(bf16[80,1024]{1,0:T(8,128)(2,1)S(1)} %shard_map.30.refs_0_), channel_id=1, source_target_pairs={{0,4},{2,6},{4,0},{6,2},{1,5},{3,7},{5,1},{7,3},{8,12},{10,14},{12... | collective-permute-start | bytes 491528 | tf_op jit(solution)/shard_map/ppermute | solution.py:21
  64.6 11.4 %collective-permute-start.29 = (bf16[2,80,1024]{2,1,0:T(8,128)(2,1)S(1)}, bf16[2,80,1024]{2,1,0:T(8,128)(2,1)S(1)}, u32[]{:S(2)}, u32[]{:S(2)}) collective-permute-start(bf16[2,80,1024]{2,1,0:T(8,128)(2,1)S(1)} %shard_map.31.near), channel_id=1, source_target_pairs={{0,6},{2,0},{4,2},{6,4},{1,7},{3,1},{5,3},{7,5},{8,14},{10,8},{12,... | collective-permute-start | bytes 983048 | tf_op jit(solution)/shard_map/ppermute | solution.py:21
  67.2 8.9 %collective-permute-start.28 = (bf16[2,80,1024]{2,1,0:T(8,128)(2,1)S(1)}, bf16[2,80,1024]{2,1,0:T(8,128)(2,1)S(1)}, u32[]{:S(2)}, u32[]{:S(2)}) collective-permute-start(bf16[2,80,1024]{2,1,0:T(8,128)(2,1)S(1)} %shard_map.31.near), channel_id=1, source_target_pairs={{0,2},{2,4},{4,6},{6,0},{1,3},{3,5},{5,7},{7,1},{8,10},{10,12},{12... | collective-permute-start | bytes 983048 | tf_op jit(solution)/shard_map/ppermute | solution.py:21
  67.2 4.5 %collective-permute-start.26 = (bf16[80,1024]{1,0:T(8,128)(2,1)S(1)}, bf16[80,1024]{1,0:T(8,128)(2,1)S(1)}, u32[]{:S(2)}, u32[]{:S(2)}) collective-permute-start(bf16[80,1024]{1,0:T(8,128)(2,1)S(1)} %collective-permute-done.25.refs_2_), channel_id=1, source_target_pairs={{0,112},{16,0},{32,16},{48,32},{64,48},{80,64},{96,80},{112,96},{1... | collective-permute-start | bytes 491528 | tf_op jit(solution)/shard_map/ppermute | solution.py:21
  67.2 5.7 %collective-permute-start.23 = (bf16[80,1024]{1,0:T(8,128)(2,1)S(1)}, bf16[80,1024]{1,0:T(8,128)(2,1)S(1)}, u32[]{:S(2)}, u32[]{:S(2)}) collective-permute-start(bf16[80,1024]{1,0:T(8,128)(2,1)S(1)} %collective-permute-done.22.refs_1_), channel_id=1, source_target_pairs={{0,16},{16,32},{32,48},{48,64},{64,80},{80,96},{96,112},{112,0},{1... | collective-permute-start | bytes 491528 | tf_op jit(solution)/shard_map/ppermute | solution.py:21
  68.7 4.5 %collective-permute-start.31 = (bf16[80,1024]{1,0:T(8,128)(2,1)S(1)}, bf16[80,1024]{1,0:T(8,128)(2,1)S(1)}, u32[]{:S(2)}, u32[]{:S(2)}) collective-permute-start(bf16[80,1024]{1,0:T(8,128)(2,1)S(1)} %collective-permute-done.30.far), channel_id=1, source_target_pairs={{0,8},{8,0},{1,9},{9,1},{2,10},{10,2},{3,11},{11,3},{4,12},{12,4},... | collective-permute-start | bytes 491528 | tf_op jit(solution)/shard_map/ppermute | solution.py:21
  71.7 6.9 %collective-permute-start.27 = (bf16[80,1024]{1,0:T(8,128)(2,1)S(1)}, bf16[80,1024]{1,0:T(8,128)(2,1)S(1)}, u32[]{:S(2)}, u32[]{:S(2)}) collective-permute-start(bf16[80,1024]{1,0:T(8,128)(2,1)S(1)} %collective-permute-done.26.refs_4_), channel_id=1, source_target_pairs={{0,112},{16,0},{32,16},{48,32},{64,48},{80,64},{96,80},{112,96},{1... | collective-permute-start | bytes 491528 | tf_op jit(solution)/shard_map/ppermute | solution.py:21
  72.9 6.4 %collective-permute-start.24 = (bf16[80,1024]{1,0:T(8,128)(2,1)S(1)}, bf16[80,1024]{1,0:T(8,128)(2,1)S(1)}, u32[]{:S(2)}, u32[]{:S(2)}) collective-permute-start(bf16[80,1024]{1,0:T(8,128)(2,1)S(1)} %collective-permute-done.23.refs_3_), channel_id=1, source_target_pairs={{0,16},{16,32},{32,48},{48,64},{64,80},{80,96},{96,112},{112,0},{1... | collective-permute-start | bytes 491528 | tf_op jit(solution)/shard_map/ppermute | solution.py:21
  73.1 8.7 %collective-permute-start.33 = (bf16[80,1024]{1,0:T(8,128)(2,1)S(1)}, bf16[80,1024]{1,0:T(8,128)(2,1)S(1)}, u32[]{:S(2)}, u32[]{:S(2)}) collective-permute-start(bf16[80,1024]{1,0:T(8,128)(2,1)S(1)} %shard_map.30.refs_0_), channel_id=1, source_target_pairs={{0,1},{1,0},{2,3},{3,2},{4,5},{5,4},{6,7},{7,6},{8,9},{9,8},{10,11... | collective-permute-start | bytes 491528 | tf_op jit(solution)/shard_map/ppermute | solution.py:21
  76.0 5.8 %collective-permute-start.35 = (bf16[80,1024]{1,0:T(8,128)(2,1)S(1)}, bf16[80,1024]{1,0:T(8,128)(2,1)S(1)}, u32[]{:S(2)}, u32[]{:S(2)}) collective-permute-start(bf16[80,1024]{1,0:T(8,128)(2,1)S(1)} %collective-permute-done.25.refs_2_), channel_id=1, source_target_pairs={{0,1},{1,0},{2,3},{3,2},{4,5},{5,4},{6,7},{7,6},{8,9},{9,8},{10,11... | collective-permute-start | bytes 491528 | tf_op jit(solution)/shard_map/ppermute | solution.py:21
  76.1 5.8 %collective-permute-start.34 = (bf16[80,1024]{1,0:T(8,128)(2,1)S(1)}, bf16[80,1024]{1,0:T(8,128)(2,1)S(1)}, u32[]{:S(2)}, u32[]{:S(2)}) collective-permute-start(bf16[80,1024]{1,0:T(8,128)(2,1)S(1)} %collective-permute-done.22.refs_1_), channel_id=1, source_target_pairs={{0,1},{1,0},{2,3},{3,2},{4,5},{5,4},{6,7},{7,6},{8,9},{9,8},{10,11... | collective-permute-start | bytes 491528 | tf_op jit(solution)/shard_map/ppermute | solution.py:21
  78.5 6.7 %collective-permute-start.37 = (bf16[80,1024]{1,0:T(8,128)(2,1)S(1)}, bf16[80,1024]{1,0:T(8,128)(2,1)S(1)}, u32[]{:S(2)}, u32[]{:S(2)}) collective-permute-start(bf16[80,1024]{1,0:T(8,128)(2,1)S(1)} %collective-permute-done.26.refs_4_), channel_id=1, source_target_pairs={{0,1},{1,0},{2,3},{3,2},{4,5},{5,4},{6,7},{7,6},{8,9},{9,8},{10,11... | collective-permute-start | bytes 491528 | tf_op jit(solution)/shard_map/ppermute | solution.py:21
  79.3 5.9 %collective-permute-start.36 = (bf16[80,1024]{1,0:T(8,128)(2,1)S(1)}, bf16[80,1024]{1,0:T(8,128)(2,1)S(1)}, u32[]{:S(2)}, u32[]{:S(2)}) collective-permute-start(bf16[80,1024]{1,0:T(8,128)(2,1)S(1)} %collective-permute-done.23.refs_3_), channel_id=1, source_target_pairs={{0,1},{1,0},{2,3},{3,2},{4,5},{5,4},{6,7},{7,6},{8,9},{9,8},{10,11... | collective-permute-start | bytes 491528 | tf_op jit(solution)/shard_map/ppermute | solution.py:21
  81.9 6.6 %collective-permute-start.32 = (bf16[80,1024]{1,0:T(8,128)(2,1)S(1)}, bf16[80,1024]{1,0:T(8,128)(2,1)S(1)}, u32[]{:S(2)}, u32[]{:S(2)}) collective-permute-start(bf16[80,1024]{1,0:T(8,128)(2,1)S(1)} %collective-permute-done.24.refs_5_), channel_id=1, source_target_pairs={{0,16},{16,32},{32,48},{48,64},{64,80},{80,96},{96,112},{112,0},{1... | collective-permute-start | bytes 491528 | tf_op jit(solution)/shard_map/ppermute | solution.py:21
  82.0 7.3 %collective-permute-start.40 = (bf16[80,1024]{1,0:T(8,128)(2,1)S(1)}, bf16[80,1024]{1,0:T(8,128)(2,1)S(1)}, u32[]{:S(2)}, u32[]{:S(2)}) collective-permute-start(bf16[80,1024]{1,0:T(8,128)(2,1)S(1)} %collective-permute-done.27.refs_6_), channel_id=1, source_target_pairs={{0,113},{1,112},{16,1},{17,0},{32,17},{33,16},{48,33},{49,32},{64,... | collective-permute-start | bytes 491528 | tf_op jit(solution)/shard_map/ppermute | solution.py:30
  (11 other events, 57.1 us)

commit v4 on v3

--- a/solution.py
+++ b/solution.py
@@ -174,8 +174,7 @@
     left, right = shift(near, "x", 1), shift(near, "x", -1)
     ynear = shift(low, Y, 1), shift(high, Y, -1)
     left, right = together(left, right)
-    far = cut(left, right)
-    far = shift(far[0], "x", 1), shift(far[1], "x", -1)
+    far = shift(low, "x", 2), shift(high, "x", 2)
     yleft, yright = shift(left, Y, 1), shift(right, Y, -1)
     *far, yleft, yright = together(*far, yleft, yright)
     yfar = together(shift(far[0], Y, 1), shift(far[1], Y, -1))

time: 123 us -> 124 us (level)
  starting transfers between devices: 45.3 us -> 47.4 us
    ppermute x40, starting transfers between devices: 42 us -> 44.2 us  [shift(): lax.ppermute(value, axis, [(i, (i + by) % count) for i in range(count)])]
    pallas_call x5 -> x4, Pallas kernels: 5.47 us -> 5.45 us  [call(): pl.pallas_call(kernel, out_shape=shapes, in_specs=[spec for spec, _ in in...]
  transfers between devices with their start and end apart: 41 -> 41, of which waited for: 11 -> 13; matrix products, arithmetic and copies ran while one was open for 0% -> 0% of each run, Pallas kernels for 0% -> 0%
where the time goes in v4:
time: 124 us
  blocking collectives  49.2 us (40%)
  starting transfers between devices  47.4 us (38%)
  waiting for transfers between devices  16.2 us (13%)
  Pallas kernels  7.19 us (6%)
  local copies, waits for them, and re-layouts  3.75 us (3%)
    ppermute x40, starting transfers between devices, shift(): lax.ppermute(value, axis, [(i, (i + by) % count) for i in range(count)])  44.2 us
    all_to_all x1, blocking collectives, per_device(): lax.all_to_all(block, ('yh', 'yl', 'x'), split_axis=0, concat_axis=0, til...  28.7 us
    all_to_all x1, blocking collectives, everywhere(): return lax.all_to_all(copies, axes, split_axis=0, concat_axis=0, tiled=True)  20.5 us
    ppermute x40, waiting for transfers between devices, shift(): lax.ppermute(value, axis, [(i, (i + by) % count) for i in range(count)])  15.4 us
    pallas_call x4, Pallas kernels, call(): pl.pallas_call(kernel, out_shape=shapes, in_specs=[spec for spec, _ in in...  5.45 us
    ppermute x1, starting transfers between devices, cross(): return lax.ppermute(value, ('z', 'c'), steps)  3.25 us
    unnamed x4, local copies, waits for them, and re-layouts  2.86 us
  transfers between devices with their start and end apart: 41, of which 13 were waited for; matrix products, arithmetic and copies ran while one was open for 0% of the time, Pallas kernels for 0%

profile of v4, /device:TPU:1, one launch (start us, length us, event | category | flops | bytes accessed | tf_op | source)
XLA Modules:
  0.0 123.8 jit_solution(16071138474781637799)
XLA Ops:
  0.9 20.5 %all_to_all.10.first.second.refs_0_ = bf16[8,80,256]{2,1,0:T(8,128)(2,1)S(1)} all-to-all(bf16[8,80,256]{2,1,0:T(8,128)(2,1)S(1)} %broadcast_in_dim.2), channel_id=1, replica_groups=mesh['yh'=2,'z'=8,'yl'=2,'x'=4,'c'=2] {'z'}, dimensions={0} | all-to-all | bytes 655360 | tf_op jit(solution)/shard_map/all_to_all | solution.py:53
  21.4 2.5 %collective-permute-start.1 = (bf16[8,80,256]{2,1,0:T(8,128)(2,1)S(1)}, bf16[8,80,256]{2,1,0:T(8,128)(2,1)S(1)}, u32[]{:S(2)}, u32[]{:S(2)}) collective-permute-start(bf16[8,80,256]{2,1,0:T(8,128)(2,1)S(1)} %all_to_all.10.first.second.refs_0_), channel_id=1, source_target_pairs={{0,6},{2,0},{4,2},{6,4},{1,7},{3,1},{5,3},{7,5},{8,14},{10,8},{12,... | collective-permute-start | bytes 983048 | tf_op jit(solution)/shard_map/ppermute | solution.py:21
  23.9 2.9 %copy-done = bf16[4,80,10240]{2,1,0:T(8,128)(2,1)S(1)} copy-done((bf16[4,80,10240]{2,1,0:T(8,128)(2,1)S(1)}, bf16[4,80,10240]{2,1,0:T(8,128)(2,1)}, u32[]{:S(2)}) %copy-start) | copy-done | bytes 6553624
  26.7 1.4 %collective-permute-start.6 = (bf16[4,80,256]{2,1,0:T(8,128)(2,1)S(1)}, bf16[4,80,256]{2,1,0:T(8,128)(2,1)S(1)}, u32[]{:S(2)}, u32[]{:S(2)}) collective-permute-start(bf16[4,80,256]{2,1,0:T(8,128)(2,1)S(1)} %get-tuple-element.27), channel_id=1, source_target_pairs={{0,8},{8,128},{128,136},{136,0},{1,9},{9,129},{129,137},{137,1},{2... | collective-permute-start | bytes 491528 | tf_op jit(solution)/shard_map/ppermute | solution.py:21
  28.3 3.1 %collective-permute-done.refs_1_ = bf16[8,80,256]{2,1,0:T(8,128)(2,1)S(1)} collective-permute-done((bf16[8,80,256]{2,1,0:T(8,128)(2,1)S(1)}, bf16[8,80,256]{2,1,0:T(8,128)(2,1)S(1)}, u32[]{:S(2)}, u32[]{:S(2)}) %collective-permute-start) | collective-permute-done | bytes 327712 | tf_op jit(solution)/shard_map/ppermute | solution.py:21
  31.4 1.3 %collective-permute-start.4 = (bf16[8,80,256]{2,1,0:T(8,128)(2,1)S(1)}, bf16[8,80,256]{2,1,0:T(8,128)(2,1)S(1)}, u32[]{:S(2)}, u32[]{:S(2)}) collective-permute-start(bf16[8,80,256]{2,1,0:T(8,128)(2,1)S(1)} %collective-permute-done.refs_1_), channel_id=1, source_target_pairs={{0,8},{8,128},{128,136},{136,0},{1,9},{9,129},{129,137},{137,1},{2... | collective-permute-start | bytes 983048 | tf_op jit(solution)/shard_map/ppermute | solution.py:21
  32.7 1.4 %collective-permute-start.5 = (bf16[8,80,256]{2,1,0:T(8,128)(2,1)S(1)}, bf16[8,80,256]{2,1,0:T(8,128)(2,1)S(1)}, u32[]{:S(2)}, u32[]{:S(2)}) collective-permute-start(bf16[8,80,256]{2,1,0:T(8,128)(2,1)S(1)} %collective-permute-done.1.refs_2_), channel_id=1, source_target_pairs={{0,136},{8,0},{128,8},{136,128},{1,137},{9,1},{129,9},{137,129},{2... | collective-permute-start | bytes 983048 | tf_op jit(solution)/shard_map/ppermute | solution.py:21
  34.2 1.5 %collective-permute-start.7 = (bf16[4,80,256]{2,1,0:T(8,128)(2,1)S(1)}, bf16[4,80,256]{2,1,0:T(8,128)(2,1)S(1)}, u32[]{:S(2)}, u32[]{:S(2)}) collective-permute-start(bf16[4,80,256]{2,1,0:T(8,128)(2,1)S(1)} %get-tuple-element.28), channel_id=1, source_target_pairs={{0,136},{8,0},{128,8},{136,128},{1,137},{9,1},{129,9},{137,129},{2... | collective-permute-start | bytes 491528 | tf_op jit(solution)/shard_map/ppermute | solution.py:21
  35.6 3.0 %collective-permute-start.3 = (bf16[4,80,256]{2,1,0:T(8,128)(2,1)S(1)}, bf16[4,80,256]{2,1,0:T(8,128)(2,1)S(1)}, u32[]{:S(2)}, u32[]{:S(2)}) collective-permute-start(bf16[4,80,256]{2,1,0:T(8,128)(2,1)S(1)} %get-tuple-element.28), channel_id=1, source_target_pairs={{0,4},{2,6},{4,0},{6,2},{1,5},{3,7},{5,1},{7,3},{8,12},{10,14},{12... | collective-permute-start | bytes 491528 | tf_op jit(solution)/shard_map/ppermute | solution.py:21
  38.6 1.2 collective-permute-done.2.refs_3_
  39.8 5.4 %collective-permute-start.10 = (bf16[8,80,256]{2,1,0:T(8,128)(2,1)S(1)}, bf16[8,80,256]{2,1,0:T(8,128)(2,1)S(1)}, u32[]{:S(2)}, u32[]{:S(2)}) collective-permute-start(bf16[8,80,256]{2,1,0:T(8,128)(2,1)S(1)} %all_to_all.10.first.second.refs_0_), channel_id=1, source_target_pairs={{0,1},{1,0},{2,3},{3,2},{4,5},{5,4},{6,7},{7,6},{8,9},{9,8},{10,11... | collective-permute-start | bytes 983048 | tf_op jit(solution)/shard_map/ppermute | solution.py:21
  45.3 1.1 collective-permute-start.15
  47.6 1.1 collective-permute-start.8
  48.7 1.7 %collective-permute-start.9 = (bf16[4,80,256]{2,1,0:T(8,128)(2,1)S(1)}, bf16[4,80,256]{2,1,0:T(8,128)(2,1)S(1)}, u32[]{:S(2)}, u32[]{:S(2)}) collective-permute-start(bf16[4,80,256]{2,1,0:T(8,128)(2,1)S(1)} %collective-permute-done.3.refs_4_), channel_id=1, source_target_pairs={{0,136},{8,0},{128,8},{136,128},{1,137},{9,1},{129,9},{137,129},{2... | collective-permute-start | bytes 491528 | tf_op jit(solution)/shard_map/ppermute | solution.py:21
  51.0 3.4 %collective-permute-done.8.refs_9_ = bf16[4,80,256]{2,1,0:T(8,128)(2,1)S(1)} collective-permute-done((bf16[4,80,256]{2,1,0:T(8,128)(2,1)S(1)}, bf16[4,80,256]{2,1,0:T(8,128)(2,1)S(1)}, u32[]{:S(2)}, u32[]{:S(2)}) %collective-permute-start.8) | collective-permute-done | bytes 163872 | tf_op jit(solution)/shard_map/ppermute | solution.py:21
  54.4 1.0 collective-permute-start.17
  57.8 2.8 %shard_map.29.refs_0_ = bf16[80,1024]{1,0:T(8,128)(2,1)S(1)} custom-call(s32[5]{0:T(128)S(1)} %stack.23.where, bf16[320,10240]{1,0:T(8,128)(2,1)S(1)} %bitcast.7, bf16[8,80,256]{2,1,0:T(8,128)(2,1)S(1)} %all_to_all.10.first.second.refs_0_, bf16[8,80,256]{2,1,0:T(8,128)(2,1)S(1)} %collective-permute-done.refs_1_, ...), custom_call_target="tpu_custom_call" | custom-call | flops 1677721600 | bytes 12582912 | tf_op jit(solution)/shard_map/pallas_call | solution.py:39
  61.1 1.5 %collective-permute-start.22 = (bf16[80,1024]{1,0:T(8,128)(2,1)S(1)}, bf16[80,1024]{1,0:T(8,128)(2,1)S(1)}, u32[]{:S(2)}, u32[]{:S(2)}) collective-permute-start(bf16[80,1024]{1,0:T(8,128)(2,1)S(1)} %shard_map.29.refs_0_), channel_id=1, source_target_pairs={{0,16},{16,32},{32,48},{48,64},{64,80},{80,96},{96,112},{112,0},{1... | collective-permute-start | bytes 491528 | tf_op jit(solution)/shard_map/ppermute | solution.py:21
  62.6 2.9 %collective-permute-start.30 = (bf16[80,1024]{1,0:T(8,128)(2,1)S(1)}, bf16[80,1024]{1,0:T(8,128)(2,1)S(1)}, u32[]{:S(2)}, u32[]{:S(2)}) collective-permute-start(bf16[80,1024]{1,0:T(8,128)(2,1)S(1)} %shard_map.29.refs_0_), channel_id=1, source_target_pairs={{0,4},{2,6},{4,0},{6,2},{1,5},{3,7},{5,1},{7,3},{8,12},{10,14},{12... | collective-permute-start | bytes 491528 | tf_op jit(solution)/shard_map/ppermute | solution.py:21
  66.1 1.6 %collective-permute-start.29 = (bf16[2,80,1024]{2,1,0:T(8,128)(2,1)S(1)}, bf16[2,80,1024]{2,1,0:T(8,128)(2,1)S(1)}, u32[]{:S(2)}, u32[]{:S(2)}) collective-permute-start(bf16[2,80,1024]{2,1,0:T(8,128)(2,1)S(1)} %shard_map.30.near), channel_id=1, source_target_pairs={{0,6},{2,0},{4,2},{6,4},{1,7},{3,1},{5,3},{7,5},{8,14},{10,8},{12,... | collective-permute-start | bytes 983048 | tf_op jit(solution)/shard_map/ppermute | solution.py:21
  69.2 1.0 collective-permute-start.31
  70.2 2.0 %collective-permute-done.26.refs_4_ = bf16[80,1024]{1,0:T(8,128)(2,1)S(1)} collective-permute-done((bf16[80,1024]{1,0:T(8,128)(2,1)S(1)}, bf16[80,1024]{1,0:T(8,128)(2,1)S(1)}, u32[]{:S(2)}, u32[]{:S(2)}) %collective-permute-start.26) | collective-permute-done | bytes 163872 | tf_op jit(solution)/shard_map/ppermute | solution.py:21
  72.2 1.9 %collective-permute-start.27 = (bf16[80,1024]{1,0:T(8,128)(2,1)S(1)}, bf16[80,1024]{1,0:T(8,128)(2,1)S(1)}, u32[]{:S(2)}, u32[]{:S(2)}) collective-permute-start(bf16[80,1024]{1,0:T(8,128)(2,1)S(1)} %collective-permute-done.26.refs_4_), channel_id=1, source_target_pairs={{0,112},{16,0},{32,16},{48,32},{64,48},{80,64},{96,80},{112,96},{1... | collective-permute-start | bytes 491528 | tf_op jit(solution)/shard_map/ppermute | solution.py:21
  74.2 2.6 %collective-permute-start.33 = (bf16[80,1024]{1,0:T(8,128)(2,1)S(1)}, bf16[80,1024]{1,0:T(8,128)(2,1)S(1)}, u32[]{:S(2)}, u32[]{:S(2)}) collective-permute-start(bf16[80,1024]{1,0:T(8,128)(2,1)S(1)} %shard_map.29.refs_0_), channel_id=1, source_target_pairs={{0,1},{1,0},{2,3},{3,2},{4,5},{5,4},{6,7},{7,6},{8,9},{9,8},{10,11... | collective-permute-start | bytes 491528 | tf_op jit(solution)/shard_map/ppermute | solution.py:21
  77.0 2.1 %collective-permute-start.34 = (bf16[80,1024]{1,0:T(8,128)(2,1)S(1)}, bf16[80,1024]{1,0:T(8,128)(2,1)S(1)}, u32[]{:S(2)}, u32[]{:S(2)}) collective-permute-start(bf16[80,1024]{1,0:T(8,128)(2,1)S(1)} %collective-permute-done.22.refs_1_), channel_id=1, source_target_pairs={{0,1},{1,0},{2,3},{3,2},{4,5},{5,4},{6,7},{7,6},{8,9},{9,8},{10,11... | collective-permute-start | bytes 491528 | tf_op jit(solution)/shard_map/ppermute | solution.py:21
  79.0 1.1 collective-permute-start.37
  80.1 3.3 %collective-permute-start.36 = (bf16[80,1024]{1,0:T(8,128)(2,1)S(1)}, bf16[80,1024]{1,0:T(8,128)(2,1)S(1)}, u32[]{:S(2)}, u32[]{:S(2)}) collective-permute-start(bf16[80,1024]{1,0:T(8,128)(2,1)S(1)} %collective-permute-done.23.refs_3_), channel_id=1, source_target_pairs={{0,1},{1,0},{2,3},{3,2},{4,5},{5,4},{6,7},{7,6},{8,9},{9,8},{10,11... | collective-permute-start | bytes 491528 | tf_op jit(solution)/shard_map/ppermute | solution.py:21
  83.5 3.2 %collective-permute-start.40 = (bf16[80,1024]{1,0:T(8,128)(2,1)S(1)}, bf16[80,1024]{1,0:T(8,128)(2,1)S(1)}, u32[]{:S(2)}, u32[]{:S(2)}) collective-permute-start(bf16[80,1024]{1,0:T(8,128)(2,1)S(1)} %collective-permute-done.27.refs_6_), channel_id=1, source_target_pairs={{0,113},{1,112},{16,1},{17,0},{32,17},{33,16},{48,33},{49,32},{64,... | collective-permute-start | bytes 491528 | tf_op jit(solution)/shard_map/ppermute | solution.py:30
  86.7 3.3 %collective-permute-done.32.refs_7_ = bf16[80,1024]{1,0:T(8,128)(2,1)S(1)} collective-permute-done((bf16[80,1024]{1,0:T(8,128)(2,1)S(1)}, bf16[80,1024]{1,0:T(8,128)(2,1)S(1)}, u32[]{:S(2)}, u32[]{:S(2)}) %collective-permute-start.32) | collective-permute-done | bytes 163872 | tf_op jit(solution)/shard_map/ppermute | solution.py:21
  90.7 2.6 %shard_map.31 = bf16[16,80,640]{2,1,0:T(8,128)(2,1)S(1)} custom-call(s32[5]{0:T(128)S(1)} %stack.23.where, bf16[2,80,1024]{2,1,0:T(8,128)(2,1)S(1)} %shard_map.30.near, bf16[2,80,1024]{2,1,0:T(8,128)(2,1)S(1)} %collective-permute-done.28.left, bf16[2,80,1024]{2,1,0:T(8,128)(2,1)S(1)} %collective-permute-done.29.right, ...), custom_call_target="tpu_custom_call" | custom-call | flops 1677721600 | bytes 6291456 | tf_op jit(solution)/shard_map/pallas_call | solution.py:39
  93.4 28.7 %all_to_all.11.pieces = bf16[16,80,640]{2,1,0:T(8,128)(2,1)S(1)} all-to-all(bf16[16,80,640]{2,1,0:T(8,128)(2,1)S(1)} %shard_map.31), channel_id=1, replica_groups=mesh['yh'=2,'z'=8,'yl'=2,'x'=4,'c'=2] {'yh','yl','x'}, dimensions={0} | all-to-all | bytes 3276800 | tf_op jit(solution)/shard_map/all_to_all | solution.py:206
  122.1 1.7 %shard_map.32 = f32[80,5120]{1,0:T(8,128)} custom-call(bf16[16,80,640]{2,1,0:T(8,128)(2,1)S(1)} %all_to_all.11.pieces), custom_call_target="tpu_custom_call" | custom-call | bytes 4194304 | tf_op jit(solution)/shard_map/pallas_call | solution.py:161
  (63 shorter events, 9.0 us)
Async XLA Ops:
  21.4 6.9 %collective-permute-start.1 = (bf16[8,80,256]{2,1,0:T(8,128)(2,1)S(1)}, bf16[8,80,256]{2,1,0:T(8,128)(2,1)S(1)}, u32[]{:S(2)}, u32[]{:S(2)}) collective-permute-start(bf16[8,80,256]{2,1,0:T(8,128)(2,1)S(1)} %all_to_all.10.first.second.refs_0_), channel_id=1, source_target_pairs={{0,6},{2,0},{4,2},{6,4},{1,7},{3,1},{5,3},{7,5},{8,14},{10,8},{12,... | collective-permute-start | bytes 983048 | tf_op jit(solution)/shard_map/ppermute | solution.py:21
  23.9 7.6 %collective-permute-start = (bf16[8,80,256]{2,1,0:T(8,128)(2,1)S(1)}, bf16[8,80,256]{2,1,0:T(8,128)(2,1)S(1)}, u32[]{:S(2)}, u32[]{:S(2)}) collective-permute-start(bf16[8,80,256]{2,1,0:T(8,128)(2,1)S(1)} %all_to_all.10.first.second.refs_0_), channel_id=1, source_target_pairs={{0,2},{2,4},{4,6},{6,0},{1,3},{3,5},{5,7},{7,1},{8,10},{10,12},{12... | collective-permute-start | bytes 983048 | tf_op jit(solution)/shard_map/ppermute | solution.py:21
  26.7 8.9 %collective-permute-start.6 = (bf16[4,80,256]{2,1,0:T(8,128)(2,1)S(1)}, bf16[4,80,256]{2,1,0:T(8,128)(2,1)S(1)}, u32[]{:S(2)}, u32[]{:S(2)}) collective-permute-start(bf16[4,80,256]{2,1,0:T(8,128)(2,1)S(1)} %get-tuple-element.27), channel_id=1, source_target_pairs={{0,8},{8,128},{128,136},{136,0},{1,9},{9,129},{129,137},{137,1},{2... | collective-permute-start | bytes 491528 | tf_op jit(solution)/shard_map/ppermute | solution.py:21
  31.4 15.6 %collective-permute-start.4 = (bf16[8,80,256]{2,1,0:T(8,128)(2,1)S(1)}, bf16[8,80,256]{2,1,0:T(8,128)(2,1)S(1)}, u32[]{:S(2)}, u32[]{:S(2)}) collective-permute-start(bf16[8,80,256]{2,1,0:T(8,128)(2,1)S(1)} %collective-permute-done.refs_1_), channel_id=1, source_target_pairs={{0,8},{8,128},{128,136},{136,0},{1,9},{9,129},{129,137},{137,1},{2... | collective-permute-start | bytes 983048 | tf_op jit(solution)/shard_map/ppermute | solution.py:21
  32.7 14.4 %collective-permute-start.5 = (bf16[8,80,256]{2,1,0:T(8,128)(2,1)S(1)}, bf16[8,80,256]{2,1,0:T(8,128)(2,1)S(1)}, u32[]{:S(2)}, u32[]{:S(2)}) collective-permute-start(bf16[8,80,256]{2,1,0:T(8,128)(2,1)S(1)} %collective-permute-done.1.refs_2_), channel_id=1, source_target_pairs={{0,136},{8,0},{128,8},{136,128},{1,137},{9,1},{129,9},{137,129},{2... | collective-permute-start | bytes 983048 | tf_op jit(solution)/shard_map/ppermute | solution.py:21
  34.2 5.7 %collective-permute-start.2 = (bf16[4,80,256]{2,1,0:T(8,128)(2,1)S(1)}, bf16[4,80,256]{2,1,0:T(8,128)(2,1)S(1)}, u32[]{:S(2)}, u32[]{:S(2)}) collective-permute-start(bf16[4,80,256]{2,1,0:T(8,128)(2,1)S(1)} %get-tuple-element.27), channel_id=1, source_target_pairs={{0,4},{2,6},{4,0},{6,2},{1,5},{3,7},{5,1},{7,3},{8,12},{10,14},{12... | collective-permute-start | bytes 491528 | tf_op jit(solution)/shard_map/ppermute | solution.py:21
  34.2 11.1 %collective-permute-start.7 = (bf16[4,80,256]{2,1,0:T(8,128)(2,1)S(1)}, bf16[4,80,256]{2,1,0:T(8,128)(2,1)S(1)}, u32[]{:S(2)}, u32[]{:S(2)}) collective-permute-start(bf16[4,80,256]{2,1,0:T(8,128)(2,1)S(1)} %get-tuple-element.28), channel_id=1, source_target_pairs={{0,136},{8,0},{128,8},{136,128},{1,137},{9,1},{129,9},{137,129},{2... | collective-permute-start | bytes 491528 | tf_op jit(solution)/shard_map/ppermute | solution.py:21
  35.6 10.7 %collective-permute-start.3 = (bf16[4,80,256]{2,1,0:T(8,128)(2,1)S(1)}, bf16[4,80,256]{2,1,0:T(8,128)(2,1)S(1)}, u32[]{:S(2)}, u32[]{:S(2)}) collective-permute-start(bf16[4,80,256]{2,1,0:T(8,128)(2,1)S(1)} %get-tuple-element.28), channel_id=1, source_target_pairs={{0,4},{2,6},{4,0},{6,2},{1,5},{3,7},{5,1},{7,3},{8,12},{10,14},{12... | collective-permute-start | bytes 491528 | tf_op jit(solution)/shard_map/ppermute | solution.py:21
  39.8 10.6 %collective-permute-start.10 = (bf16[8,80,256]{2,1,0:T(8,128)(2,1)S(1)}, bf16[8,80,256]{2,1,0:T(8,128)(2,1)S(1)}, u32[]{:S(2)}, u32[]{:S(2)}) collective-permute-start(bf16[8,80,256]{2,1,0:T(8,128)(2,1)S(1)} %all_to_all.10.first.second.refs_0_), channel_id=1, source_target_pairs={{0,1},{1,0},{2,3},{3,2},{4,5},{5,4},{6,7},{7,6},{8,9},{9,8},{10,11... | collective-permute-start | bytes 983048 | tf_op jit(solution)/shard_map/ppermute | solution.py:21
  47.1 8.4 %collective-permute-start.11 = (bf16[8,80,256]{2,1,0:T(8,128)(2,1)S(1)}, bf16[8,80,256]{2,1,0:T(8,128)(2,1)S(1)}, u32[]{:S(2)}, u32[]{:S(2)}) collective-permute-start(bf16[8,80,256]{2,1,0:T(8,128)(2,1)S(1)} %collective-permute-done.refs_1_), channel_id=1, source_target_pairs={{0,1},{1,0},{2,3},{3,2},{4,5},{5,4},{6,7},{7,6},{8,9},{9,8},{10,11... | collective-permute-start | bytes 983048 | tf_op jit(solution)/shard_map/ppermute | solution.py:21
  47.1 8.9 %collective-permute-start.12 = (bf16[8,80,256]{2,1,0:T(8,128)(2,1)S(1)}, bf16[8,80,256]{2,1,0:T(8,128)(2,1)S(1)}, u32[]{:S(2)}, u32[]{:S(2)}) collective-permute-start(bf16[8,80,256]{2,1,0:T(8,128)(2,1)S(1)} %collective-permute-done.1.refs_2_), channel_id=1, source_target_pairs={{0,1},{1,0},{2,3},{3,2},{4,5},{5,4},{6,7},{7,6},{8,9},{9,8},{10,11... | collective-permute-start | bytes 983048 | tf_op jit(solution)/shard_map/ppermute | solution.py:21
  47.6 6.9 %collective-permute-start.8 = (bf16[4,80,256]{2,1,0:T(8,128)(2,1)S(1)}, bf16[4,80,256]{2,1,0:T(8,128)(2,1)S(1)}, u32[]{:S(2)}, u32[]{:S(2)}) collective-permute-start(bf16[4,80,256]{2,1,0:T(8,128)(2,1)S(1)} %collective-permute-done.2.refs_3_), channel_id=1, source_target_pairs={{0,8},{8,128},{128,136},{136,0},{1,9},{9,129},{129,137},{137,1},{2... | collective-permute-start | bytes 491528 | tf_op jit(solution)/shard_map/ppermute | solution.py:21
  48.7 6.7 %collective-permute-start.9 = (bf16[4,80,256]{2,1,0:T(8,128)(2,1)S(1)}, bf16[4,80,256]{2,1,0:T(8,128)(2,1)S(1)}, u32[]{:S(2)}, u32[]{:S(2)}) collective-permute-start(bf16[4,80,256]{2,1,0:T(8,128)(2,1)S(1)} %collective-permute-done.3.refs_4_), channel_id=1, source_target_pairs={{0,136},{8,0},{128,8},{136,128},{1,137},{9,1},{129,9},{137,129},{2... | collective-permute-start | bytes 491528 | tf_op jit(solution)/shard_map/ppermute | solution.py:21
  50.4 5.8 %collective-permute-start.13 = (bf16[4,80,256]{2,1,0:T(8,128)(2,1)S(1)}, bf16[4,80,256]{2,1,0:T(8,128)(2,1)S(1)}, u32[]{:S(2)}, u32[]{:S(2)}) collective-permute-start(bf16[4,80,256]{2,1,0:T(8,128)(2,1)S(1)} %collective-permute-done.2.refs_3_), channel_id=1, source_target_pairs={{0,1},{1,0},{2,3},{3,2},{4,5},{5,4},{6,7},{7,6},{8,9},{9,8},{10,11... | collective-permute-start | bytes 491528 | tf_op jit(solution)/shard_map/ppermute | solution.py:21
  60.6 5.5 %collective-permute-start.21 = (bf16[80,1024]{1,0:T(8,128)(2,1)S(1)}, bf16[80,1024]{1,0:T(8,128)(2,1)S(1)}, u32[]{:S(2)}, u32[]{:S(2)}) collective-permute-start(bf16[80,1024]{1,0:T(8,128)(2,1)S(1)} %shard_map.29.refs_0_), channel_id=1, source_target_pairs={{0,8},{8,0},{1,9},{9,1},{2,10},{10,2},{3,11},{11,3},{4,12},{12,4},... | collective-permute-start | bytes 491528 | tf_op jit(solution)/shard_map/ppermute | solution.py:21
  61.1 6.6 %collective-permute-start.25 = (bf16[80,1024]{1,0:T(8,128)(2,1)S(1)}, bf16[80,1024]{1,0:T(8,128)(2,1)S(1)}, u32[]{:S(2)}, u32[]{:S(2)}) collective-permute-start(bf16[80,1024]{1,0:T(8,128)(2,1)S(1)} %shard_map.29.refs_0_), channel_id=1, source_target_pairs={{0,112},{16,0},{32,16},{48,32},{64,48},{80,64},{96,80},{112,96},{1... | collective-permute-start | bytes 491528 | tf_op jit(solution)/shard_map/ppermute | solution.py:21
  61.1 7.3 %collective-permute-start.22 = (bf16[80,1024]{1,0:T(8,128)(2,1)S(1)}, bf16[80,1024]{1,0:T(8,128)(2,1)S(1)}, u32[]{:S(2)}, u32[]{:S(2)}) collective-permute-start(bf16[80,1024]{1,0:T(8,128)(2,1)S(1)} %shard_map.29.refs_0_), channel_id=1, source_target_pairs={{0,16},{16,32},{32,48},{48,64},{64,80},{80,96},{96,112},{112,0},{1... | collective-permute-start | bytes 491528 | tf_op jit(solution)/shard_map/ppermute | solution.py:21
  62.6 6.6 %collective-permute-start.30 = (bf16[80,1024]{1,0:T(8,128)(2,1)S(1)}, bf16[80,1024]{1,0:T(8,128)(2,1)S(1)}, u32[]{:S(2)}, u32[]{:S(2)}) collective-permute-start(bf16[80,1024]{1,0:T(8,128)(2,1)S(1)} %shard_map.29.refs_0_), channel_id=1, source_target_pairs={{0,4},{2,6},{4,0},{6,2},{1,5},{3,7},{5,1},{7,3},{8,12},{10,14},{12... | collective-permute-start | bytes 491528 | tf_op jit(solution)/shard_map/ppermute | solution.py:21
  66.1 10.7 %collective-permute-start.29 = (bf16[2,80,1024]{2,1,0:T(8,128)(2,1)S(1)}, bf16[2,80,1024]{2,1,0:T(8,128)(2,1)S(1)}, u32[]{:S(2)}, u32[]{:S(2)}) collective-permute-start(bf16[2,80,1024]{2,1,0:T(8,128)(2,1)S(1)} %shard_map.30.near), channel_id=1, source_target_pairs={{0,6},{2,0},{4,2},{6,4},{1,7},{3,1},{5,3},{7,5},{8,14},{10,8},{12,... | collective-permute-start | bytes 983048 | tf_op jit(solution)/shard_map/ppermute | solution.py:21
  67.7 9.3 %collective-permute-start.28 = (bf16[2,80,1024]{2,1,0:T(8,128)(2,1)S(1)}, bf16[2,80,1024]{2,1,0:T(8,128)(2,1)S(1)}, u32[]{:S(2)}, u32[]{:S(2)}) collective-permute-start(bf16[2,80,1024]{2,1,0:T(8,128)(2,1)S(1)} %shard_map.30.near), channel_id=1, source_target_pairs={{0,2},{2,4},{4,6},{6,0},{1,3},{3,5},{5,7},{7,1},{8,10},{10,12},{12... | collective-permute-start | bytes 983048 | tf_op jit(solution)/shard_map/ppermute | solution.py:21
  67.7 4.5 %collective-permute-start.26 = (bf16[80,1024]{1,0:T(8,128)(2,1)S(1)}, bf16[80,1024]{1,0:T(8,128)(2,1)S(1)}, u32[]{:S(2)}, u32[]{:S(2)}) collective-permute-start(bf16[80,1024]{1,0:T(8,128)(2,1)S(1)} %collective-permute-done.25.refs_2_), channel_id=1, source_target_pairs={{0,112},{16,0},{32,16},{48,32},{64,48},{80,64},{96,80},{112,96},{1... | collective-permute-start | bytes 491528 | tf_op jit(solution)/shard_map/ppermute | solution.py:21
  68.5 5.7 %collective-permute-start.23 = (bf16[80,1024]{1,0:T(8,128)(2,1)S(1)}, bf16[80,1024]{1,0:T(8,128)(2,1)S(1)}, u32[]{:S(2)}, u32[]{:S(2)}) collective-permute-start(bf16[80,1024]{1,0:T(8,128)(2,1)S(1)} %collective-permute-done.22.refs_1_), channel_id=1, source_target_pairs={{0,16},{16,32},{32,48},{48,64},{64,80},{80,96},{96,112},{112,0},{1... | collective-permute-start | bytes 491528 | tf_op jit(solution)/shard_map/ppermute | solution.py:21
  69.2 5.0 %collective-permute-start.31 = (bf16[80,1024]{1,0:T(8,128)(2,1)S(1)}, bf16[80,1024]{1,0:T(8,128)(2,1)S(1)}, u32[]{:S(2)}, u32[]{:S(2)}) collective-permute-start(bf16[80,1024]{1,0:T(8,128)(2,1)S(1)} %collective-permute-done.30.far), channel_id=1, source_target_pairs={{0,8},{8,0},{1,9},{9,1},{2,10},{10,2},{3,11},{11,3},{4,12},{12,4},... | collective-permute-start | bytes 491528 | tf_op jit(solution)/shard_map/ppermute | solution.py:21
  72.2 6.9 %collective-permute-start.27 = (bf16[80,1024]{1,0:T(8,128)(2,1)S(1)}, bf16[80,1024]{1,0:T(8,128)(2,1)S(1)}, u32[]{:S(2)}, u32[]{:S(2)}) collective-permute-start(bf16[80,1024]{1,0:T(8,128)(2,1)S(1)} %collective-permute-done.26.refs_4_), channel_id=1, source_target_pairs={{0,112},{16,0},{32,16},{48,32},{64,48},{80,64},{96,80},{112,96},{1... | collective-permute-start | bytes 491528 | tf_op jit(solution)/shard_map/ppermute | solution.py:21
  74.2 5.9 %collective-permute-start.24 = (bf16[80,1024]{1,0:T(8,128)(2,1)S(1)}, bf16[80,1024]{1,0:T(8,128)(2,1)S(1)}, u32[]{:S(2)}, u32[]{:S(2)}) collective-permute-start(bf16[80,1024]{1,0:T(8,128)(2,1)S(1)} %collective-permute-done.23.refs_3_), channel_id=1, source_target_pairs={{0,16},{16,32},{32,48},{48,64},{64,80},{80,96},{96,112},{112,0},{1... | collective-permute-start | bytes 491528 | tf_op jit(solution)/shard_map/ppermute | solution.py:21
  74.2 9.1 %collective-permute-start.33 = (bf16[80,1024]{1,0:T(8,128)(2,1)S(1)}, bf16[80,1024]{1,0:T(8,128)(2,1)S(1)}, u32[]{:S(2)}, u32[]{:S(2)}) collective-permute-start(bf16[80,1024]{1,0:T(8,128)(2,1)S(1)} %shard_map.29.refs_0_), channel_id=1, source_target_pairs={{0,1},{1,0},{2,3},{3,2},{4,5},{5,4},{6,7},{7,6},{8,9},{9,8},{10,11... | collective-permute-start | bytes 491528 | tf_op jit(solution)/shard_map/ppermute | solution.py:21
  76.9 6.5 %collective-permute-start.35 = (bf16[80,1024]{1,0:T(8,128)(2,1)S(1)}, bf16[80,1024]{1,0:T(8,128)(2,1)S(1)}, u32[]{:S(2)}, u32[]{:S(2)}) collective-permute-start(bf16[80,1024]{1,0:T(8,128)(2,1)S(1)} %collective-permute-done.25.refs_2_), channel_id=1, source_target_pairs={{0,1},{1,0},{2,3},{3,2},{4,5},{5,4},{6,7},{7,6},{8,9},{9,8},{10,11... | collective-permute-start | bytes 491528 | tf_op jit(solution)/shard_map/ppermute | solution.py:21
  77.0 6.5 %collective-permute-start.34 = (bf16[80,1024]{1,0:T(8,128)(2,1)S(1)}, bf16[80,1024]{1,0:T(8,128)(2,1)S(1)}, u32[]{:S(2)}, u32[]{:S(2)}) collective-permute-start(bf16[80,1024]{1,0:T(8,128)(2,1)S(1)} %collective-permute-done.22.refs_1_), channel_id=1, source_target_pairs={{0,1},{1,0},{2,3},{3,2},{4,5},{5,4},{6,7},{7,6},{8,9},{9,8},{10,11... | collective-permute-start | bytes 491528 | tf_op jit(solution)/shard_map/ppermute | solution.py:21
  79.0 7.7 %collective-permute-start.37 = (bf16[80,1024]{1,0:T(8,128)(2,1)S(1)}, bf16[80,1024]{1,0:T(8,128)(2,1)S(1)}, u32[]{:S(2)}, u32[]{:S(2)}) collective-permute-start(bf16[80,1024]{1,0:T(8,128)(2,1)S(1)} %collective-permute-done.26.refs_4_), channel_id=1, source_target_pairs={{0,1},{1,0},{2,3},{3,2},{4,5},{5,4},{6,7},{7,6},{8,9},{9,8},{10,11... | collective-permute-start | bytes 491528 | tf_op jit(solution)/shard_map/ppermute | solution.py:21
  80.1 6.6 %collective-permute-start.36 = (bf16[80,1024]{1,0:T(8,128)(2,1)S(1)}, bf16[80,1024]{1,0:T(8,128)(2,1)S(1)}, u32[]{:S(2)}, u32[]{:S(2)}) collective-permute-start(bf16[80,1024]{1,0:T(8,128)(2,1)S(1)} %collective-permute-done.23.refs_3_), channel_id=1, source_target_pairs={{0,1},{1,0},{2,3},{3,2},{4,5},{5,4},{6,7},{7,6},{8,9},{9,8},{10,11... | collective-permute-start | bytes 491528 | tf_op jit(solution)/shard_map/ppermute | solution.py:21
  83.4 6.6 %collective-permute-start.32 = (bf16[80,1024]{1,0:T(8,128)(2,1)S(1)}, bf16[80,1024]{1,0:T(8,128)(2,1)S(1)}, u32[]{:S(2)}, u32[]{:S(2)}) collective-permute-start(bf16[80,1024]{1,0:T(8,128)(2,1)S(1)} %collective-permute-done.24.refs_5_), channel_id=1, source_target_pairs={{0,16},{16,32},{32,48},{48,64},{64,80},{80,96},{96,112},{112,0},{1... | collective-permute-start | bytes 491528 | tf_op jit(solution)/shard_map/ppermute | solution.py:21
  83.5 7.3 %collective-permute-start.40 = (bf16[80,1024]{1,0:T(8,128)(2,1)S(1)}, bf16[80,1024]{1,0:T(8,128)(2,1)S(1)}, u32[]{:S(2)}, u32[]{:S(2)}) collective-permute-start(bf16[80,1024]{1,0:T(8,128)(2,1)S(1)} %collective-permute-done.27.refs_6_), channel_id=1, source_target_pairs={{0,113},{1,112},{16,1},{17,0},{32,17},{33,16},{48,33},{49,32},{64,... | collective-permute-start | bytes 491528 | tf_op jit(solution)/shard_map/ppermute | solution.py:30
  (11 other events, 57.1 us)
